TPU v7x, 256 devices: a whole 4x4x8 slice. The times are simulated.
256 devices in a mesh: region: 32 (over y, x, core), block: 8 (over z).
Axes of the slice: x: 4, y: 4, z: 8, core: 2. Of those that a mesh axis runs over, the one named last changes fastest.
Arguments:
- right_side: float32 [768, 512, 256], P('region', 'block'), may hold values from -6 to 6
- knudsen: float32 [768, 512, 256], P('region', 'block'), may hold values from 0.1 to 1
- solid: int32 [768, 512, 256], P('region', 'block'), may hold values 0 or 1
Outputs:
- concentration: float32 [768, 512, 256], P('region', 'block')
Inputs may be any that keep to these rules, and one draw needn't show every extreme that they name: 1 marks a solid voxel, 0 a pore.
All inputs are finite; a program needn't handle non-finite values. No bound on the sum of `solid` on one device may be relied on, other than what follows from the above.
Results may differ from a plain program's by a relative error of at most 0.00002.
Values sent between devices are 32-bit elements; how exact they have to be, the bound alone decides.
A program may use at most 128 MiB of HBM per device.

v0:
```python
import jax
import jax.numpy as jnp
from jax import lax
from jax.sharding import PartitionSpec as P

COARSEN = 8
PRE_SWEEPS = 3
POST_SWEEPS = 3
COARSE_SWEEPS = 6


MASS_TERM = 0.05
RELAX_WEIGHT = 0.8


def padded_2(cells, sides, width):
    for axis, dim in sides:
        count = lax.axis_size(axis)
        ends = count - 1
        head = lax.slice_in_dim(cells, 0, width, axis=dim)
        tail = lax.slice_in_dim(cells, cells.shape[dim] - width, cells.shape[dim], axis=dim)
        cells = jnp.concatenate(
            [
                lax.ppermute(tail, axis, [(i, (i + 1) % count) for i in range(ends)]),
                cells,
                lax.ppermute(head, axis, [((i + 1) % count, i) for i in range(ends)]),
            ],
            axis=dim,
        )
    return cells


def neighbours(padded):
    center = padded[1:-1, 1:-1, :]
    along_z = jnp.pad(center, ((0, 0), (0, 0), (1, 1)))
    total = padded[2:, 1:-1, :] + padded[:-2, 1:-1, :]
    total = total + padded[1:-1, 2:, :] + padded[1:-1, :-2, :]
    return total + along_z[:, :, 2:] + along_z[:, :, :-2]


def aggregate(values):
    dims = values.shape
    shaped = values.reshape(
        dims[0] // COARSEN, COARSEN, dims[1] // COARSEN, COARSEN, dims[2] // COARSEN, COARSEN
    )
    return shaped.sum(axis=(1, 3, 5))


def coarse_operator(coef_pad, pore_mask, residual):
    dims = pore_mask.shape
    inner = coef_pad[1:-1, 1:-1, :]
    face_x = (coef_pad[1:, 1:-1, :] * coef_pad[:-1, 1:-1, :])[::COARSEN]
    cond_x = face_x.reshape(
        face_x.shape[0], dims[1] // COARSEN, COARSEN, dims[2] // COARSEN, COARSEN
    ).sum(axis=(2, 4))
    face_y = (coef_pad[1:-1, 1:, :] * coef_pad[1:-1, :-1, :])[:, ::COARSEN]
    cond_y = face_y.reshape(
        dims[0] // COARSEN, COARSEN, face_y.shape[1], dims[2] // COARSEN, COARSEN
    ).sum(axis=(1, 4))
    padded_z = jnp.pad(inner, ((0, 0), (0, 0), (1, 1)))
    face_z = (padded_z[:, :, 1:] * padded_z[:, :, :-1])[:, :, ::COARSEN]
    cond_z = face_z.reshape(
        dims[0] // COARSEN, COARSEN, dims[1] // COARSEN, COARSEN, face_z.shape[2]
    ).sum(axis=(1, 3))
    count = aggregate(pore_mask)
    coarse_residual = aggregate(residual)
    coarse_diag = (
        MASS_TERM * (count + 1.0)
        + cond_x[:-1]
        + cond_x[1:]
        + cond_y[:, :-1]
        + cond_y[:, 1:]
        + cond_z[:, :, :-1]
        + cond_z[:, :, 1:]
    )
    return jnp.stack(
        [
            coarse_residual,
            coarse_diag,
            cond_x[:-1],
            cond_x[1:],
            cond_y[:, :-1],
            cond_y[:, 1:],
            cond_z[:, :, :-1],
            cond_z[:, :, 1:],
        ]
    )


def coarse_relax(stacked, pad_coarse):
    coarse_residual = stacked[0]
    coarse_diag = stacked[1]
    correction = RELAX_WEIGHT * coarse_residual / coarse_diag
    for sweep_index in range(COARSE_SWEEPS - 1):
        padded = pad_coarse(correction)
        padded_z = jnp.pad(correction, ((0, 0), (0, 0), (1, 1)))
        offdiag = stacked[2] * padded[:-2, 1:-1] + stacked[3] * padded[2:, 1:-1]
        offdiag = offdiag + stacked[4] * padded[1:-1, :-2] + stacked[5] * padded[1:-1, 2:]
        offdiag = offdiag + stacked[6] * padded_z[:, :, :-2] + stacked[7] * padded_z[:, :, 2:]
        correction = (
            correction
            + RELAX_WEIGHT * (coarse_residual - coarse_diag * correction + offdiag) / coarse_diag
        )
    return correction


def prolong(correction):
    dims = correction.shape
    wide = jnp.broadcast_to(
        correction[:, None, :, None, :, None],
        (dims[0], COARSEN, dims[1], COARSEN, dims[2], COARSEN),
    )
    return wide.reshape(dims[0] * COARSEN, dims[1] * COARSEN, dims[2] * COARSEN)


def solve_coarse(stacked):

    def pad_sharded(values):
        return padded_2(values, (("region", 0), ("block", 1)), 1)

    return coarse_relax(stacked, pad_sharded)


def shards(right_side, knudsen, solid):
    pore_mask = (1 - solid).astype(jnp.float32)
    root_coef = jnp.sqrt(knudsen * pore_mask)
    source = right_side * pore_mask
    coef_pad = padded_2(root_coef, (("region", 0), ("block", 1)), 1)
    diagonal = pore_mask * (MASS_TERM + root_coef * neighbours(coef_pad)) + (1.0 - pore_mask)
    inv_diag = 1.0 / diagonal
    scaled = source * inv_diag

    def coupling(iterate):
        padded = padded_2(root_coef * iterate, (("region", 0), ("block", 1)), 1)
        return root_coef * neighbours(padded)

    iterate = RELAX_WEIGHT * scaled
    for sweep_index in range(PRE_SWEEPS - 1):
        iterate = iterate + RELAX_WEIGHT * (scaled - iterate + inv_diag * coupling(iterate))
    residual = source - diagonal * iterate + coupling(iterate)
    stacked = coarse_operator(coef_pad, pore_mask, residual)
    iterate = iterate + pore_mask * prolong(solve_coarse(stacked))
    for sweep_index in range(POST_SWEEPS):
        iterate = iterate + RELAX_WEIGHT * (scaled - iterate + inv_diag * coupling(iterate))
    return iterate


def solution(mesh):
    placed = (P("region", "block", None), P("region", "block", None), P("region", "block", None))
    return jax.shard_map(
        shards, mesh=mesh, in_specs=placed, out_specs=P("region", "block", None), check_vma=False
    )
```

profile of v0, /device:TPU:135, one launch (start us, length us, event | category | flops | bytes accessed | tf_op | source)
XLA Modules:
  0.0 382.7 jit_solution(12660433651348121142)
XLA Ops:
  0.0 2.4 multiply_sqrt_fusion
  2.4 3.7 collective-permute-start.1
  8.0 5.8 %collective-permute-done = f32[1,64,256]{2,1,0:T(8,128)S(1)} collective-permute-done((f32[1,64,256]{2,1,0:T(8,128)S(1)}, f32[1,64,256]{2,1,0:T(8,128)S(1)}, u32[]{:S(2)}, u32[]{:S(2)}) %collective-permute-start) | collective-permute-done | bytes 65568 | tf_op jit(solution)/shard_map/ppermute | solution.py:26
  15.8 3.6 collective-permute-start.3
  19.4 2.4 collective-permute-done.3
  24.2 3.1 collective-permute-start.5
  29.2 5.8 %collective-permute-done.4 = f32[1,64,256]{2,1,0:T(8,128)S(1)} collective-permute-done((f32[1,64,256]{2,1,0:T(8,128)S(1)}, f32[1,64,256]{2,1,0:T(8,128)S(1)}, u32[]{:S(2)}, u32[]{:S(2)}) %collective-permute-start.4) | collective-permute-done | bytes 65568 | tf_op jit(solution)/shard_map/ppermute | solution.py:26
  36.9 3.4 collective-permute-start.7
  42.8 3.1 fusion.70
  47.7 3.0 collective-permute-start.9
  52.6 2.1 fusion
  54.7 8.6 %slice.509 = f32[24,64,33]{2,1,0:T(8,128)} slice(f32[24,64,257]{2,1,0:T(8,128)} %fusion), slice={[0:24:1], [0:64:1], [0:257:8]} | slice | bytes 405504 | tf_op jit(solution)/shard_map/slice | solution.py:61
  63.2 17.3 %reshape.20 = f32[3,8,8,8,32,8]{5,4,3,2,1,0:T(8,128)} reshape(f32[24,64,256]{2,1,0:T(8,128)} %subtract_convert_fusion) | data formatting | bytes 3145728 | tf_op jit(solution)/shard_map/reshape | solution.py:43
  81.7 10.1 %reduce_sum.46 = f32[3,8,32]{2,1,0:T(8,128)} reduce(f32[3,8,8,8,32,8]{5,4,3,2,1,0:T(8,128)} %reshape.20, f32[]{:T(128)} %constant.7.clone.1), dimensions={1,3,5}, to_apply=%region_1.2 | reduce | flops 392448 | bytes 1575940 | tf_op jit(solution)/shard_map/reduce_sum | solution.py:46
  95.5 3.4 collective-permute-start.11
  99.1 3.7 reshape.21
  102.8 2.6 reduce_sum.47
  105.5 14.0 %fusion.143 = (f32[24,64,256]{2,1,0:T(8,128)S(1)}, f32[24,64,256]{2,1,0:T(8,128)}) fusion(f32[24,64,256]{2,1,0:T(8,128)S(1)} %multiply_sqrt_fusion, f32[24,64,256]{2,1,0:T(8,128)} %copy-done.7, f32[1,64,256]{2,1,0:T(8,128)S(1)} %copy-done.18, f32[1,64,256]{2,1,0:T(8,128)S(1)} %copy-done.16, f32[26,1,256]{2,1,0:T(1,128)} %collective-permute-done.11, ...), kind=kLoop, calls=%fused_computation.299 | loop fusion | flops 16515072 | bytes 11378688 | tf_op jit(solution)/shard_map/mul | solution.py:134
  121.2 6.3 %collective-permute-start.13 = (f32[1,64,256]{2,1,0:T(8,128)}, f32[1,64,256]{2,1,0:T(8,128)S(1)}, u32[]{:S(2)}, u32[]{:S(2)}) collective-permute-start(f32[1,64,256]{2,1,0:T(8,128)} %get-tuple-element.38), channel_id=1, source_target_pairs={{0,8},{8,16},{16,24},{24,32},{32,40},{40,48},{48,56},{56,64},{64,7... | collective-permute-start | bytes 196616 | tf_op jit(solution)/shard_map/ppermute | solution.py:24
  127.5 2.1 collective-permute-start.12
  131.1 3.3 slice.504
  135.6 3.7 reshape.22
  139.3 2.3 reduce_sum.48
  142.8 2.9 collective-permute-start.14
  145.7 2.4 collective-permute-start.15
  148.2 3.3 collective-permute-done.15
  151.5 8.2 %fusion.29 = f32[24,64,256]{2,1,0:T(8,128)} fusion(f32[24,64,256]{2,1,0:T(8,128)S(1)} %multiply_sqrt_fusion, f32[24,64,256]{2,1,0:T(8,128)} %copy-done.8, f32[26,1,256]{2,1,0:T(1,128)S(1)} %collective-permute-done.15, f32[1,64,256]{2,1,0:T(8,128)S(1)} %collective-permute-done.12, f32[1,64,256]{2,1,0:T(8,128)S(1)} %collective-permute-done.13, ...), kind=kLoop, calls=%fused_computation.57 | loop fusion | flops 6684672 | bytes 9621504 | tf_op jit(solution)/shard_map/add | solution.py:140
  159.7 17.3 %reshape.19 = f32[3,8,8,8,32,8]{5,4,3,2,1,0:T(8,128)} reshape(f32[24,64,256]{2,1,0:T(8,128)} %fusion.29) | data formatting | bytes 3145728 | tf_op jit(solution)/shard_map/reshape | solution.py:43
  176.9 9.5 %reduce_sum.45 = f32[3,8,32]{2,1,0:T(8,128)S(1)} reduce(f32[3,8,8,8,32,8]{5,4,3,2,1,0:T(8,128)} %reshape.19, f32[]{:T(128)} %constant.7.clone.1), dimensions={1,3,5}, to_apply=%region_0.1 | reduce | flops 392448 | bytes 1575940 | tf_op jit(solution)/shard_map/reduce_sum | solution.py:46
  186.5 7.2 %collective-permute-start.16 = (f32[1,8,32]{2,1,0:T(8,128)S(1)}, f32[1,8,32]{2,1,0:T(8,128)S(1)}, u32[]{:S(2)}, u32[]{:S(2)}) collective-permute-start(f32[1,8,32]{2,1,0:T(8,128)S(1)} %get-tuple-element.66), channel_id=1, source_target_pairs={{0,8},{8,16},{16,24},{24,32},{32,40},{40,48},{48,56},{56,64},{64,7... | collective-permute-start | bytes 3080 | tf_op jit(solution)/shard_map/ppermute | solution.py:24
  195.7 5.1 %collective-permute-done.17 = f32[1,8,32]{2,1,0:T(8,128)S(1)} collective-permute-done((f32[1,8,32]{2,1,0:T(8,128)S(1)}, f32[1,8,32]{2,1,0:T(8,128)S(1)}, u32[]{:S(2)}, u32[]{:S(2)}) %collective-permute-start.17) | collective-permute-done | bytes 1056 | tf_op jit(solution)/shard_map/ppermute | solution.py:26
  202.7 4.6 %collective-permute-start.19 = (f32[5,1,32]{2,1,0:T(1,128)S(1)}, f32[5,1,32]{2,1,0:T(1,128)S(1)}, u32[]{:S(2)}, u32[]{:S(2)}) collective-permute-start(f32[5,1,32]{2,1,0:T(1,128)S(1)} %get-tuple-element.55), channel_id=1, source_target_pairs={{1,0},{2,1},{3,2},{4,3},{5,4},{6,5},{7,6},{9,8},{10,9},{11,10},{12... | collective-permute-start | bytes 1928 | tf_op jit(solution)/shard_map/ppermute | solution.py:26
  208.1 3.1 collective-permute-start.20
  211.2 1.9 collective-permute-start.21
  213.1 5.1 %collective-permute-done.21 = f32[1,8,32]{2,1,0:T(8,128)S(1)} collective-permute-done((f32[1,8,32]{2,1,0:T(8,128)S(1)}, f32[1,8,32]{2,1,0:T(8,128)S(1)}, u32[]{:S(2)}, u32[]{:S(2)}) %collective-permute-start.21) | collective-permute-done | bytes 1056 | tf_op jit(solution)/shard_map/ppermute | solution.py:26
  218.2 1.9 collective-permute-start.22
  220.1 5.1 %collective-permute-start.23 = (f32[5,1,32]{2,1,0:T(1,128)S(1)}, f32[5,1,32]{2,1,0:T(1,128)S(1)}, u32[]{:S(2)}, u32[]{:S(2)}) collective-permute-start(f32[5,1,32]{2,1,0:T(1,128)S(1)} %get-tuple-element.53), channel_id=1, source_target_pairs={{1,0},{2,1},{3,2},{4,3},{5,4},{6,5},{7,6},{9,8},{10,9},{11,10},{12... | collective-permute-start | bytes 1928 | tf_op jit(solution)/shard_map/ppermute | solution.py:26
  226.1 2.8 collective-permute-start.24
  230.8 5.1 %collective-permute-done.25 = f32[1,8,32]{2,1,0:T(8,128)S(1)} collective-permute-done((f32[1,8,32]{2,1,0:T(8,128)S(1)}, f32[1,8,32]{2,1,0:T(8,128)S(1)}, u32[]{:S(2)}, u32[]{:S(2)}) %collective-permute-start.25) | collective-permute-done | bytes 1056 | tf_op jit(solution)/shard_map/ppermute | solution.py:26
  237.9 5.1 %collective-permute-start.27 = (f32[5,1,32]{2,1,0:T(1,128)S(1)}, f32[5,1,32]{2,1,0:T(1,128)S(1)}, u32[]{:S(2)}, u32[]{:S(2)}) collective-permute-start(f32[5,1,32]{2,1,0:T(1,128)S(1)} %get-tuple-element.51), channel_id=1, source_target_pairs={{1,0},{2,1},{3,2},{4,3},{5,4},{6,5},{7,6},{9,8},{10,9},{11,10},{12... | collective-permute-start | bytes 1928 | tf_op jit(solution)/shard_map/ppermute | solution.py:26
  243.8 2.8 collective-permute-start.28
  248.5 5.1 %collective-permute-done.29 = f32[1,8,32]{2,1,0:T(8,128)S(1)} collective-permute-done((f32[1,8,32]{2,1,0:T(8,128)S(1)}, f32[1,8,32]{2,1,0:T(8,128)S(1)}, u32[]{:S(2)}, u32[]{:S(2)}) %collective-permute-start.29) | collective-permute-done | bytes 1056 | tf_op jit(solution)/shard_map/ppermute | solution.py:26
  255.6 5.1 %collective-permute-start.31 = (f32[5,1,32]{2,1,0:T(1,128)S(1)}, f32[5,1,32]{2,1,0:T(1,128)S(1)}, u32[]{:S(2)}, u32[]{:S(2)}) collective-permute-start(f32[5,1,32]{2,1,0:T(1,128)S(1)} %get-tuple-element.49), channel_id=1, source_target_pairs={{1,0},{2,1},{3,2},{4,3},{5,4},{6,5},{7,6},{9,8},{10,9},{11,10},{12... | collective-permute-start | bytes 1928 | tf_op jit(solution)/shard_map/ppermute | solution.py:26
  261.5 2.8 collective-permute-start.32
  266.2 5.1 %collective-permute-done.33 = f32[1,8,32]{2,1,0:T(8,128)S(1)} collective-permute-done((f32[1,8,32]{2,1,0:T(8,128)S(1)}, f32[1,8,32]{2,1,0:T(8,128)S(1)}, u32[]{:S(2)}, u32[]{:S(2)}) %collective-permute-start.33) | collective-permute-done | bytes 1056 | tf_op jit(solution)/shard_map/ppermute | solution.py:26
  273.3 5.1 %collective-permute-start.35 = (f32[5,1,32]{2,1,0:T(1,128)S(1)}, f32[5,1,32]{2,1,0:T(1,128)S(1)}, u32[]{:S(2)}, u32[]{:S(2)}) collective-permute-start(f32[5,1,32]{2,1,0:T(1,128)S(1)} %get-tuple-element.47), channel_id=1, source_target_pairs={{1,0},{2,1},{3,2},{4,3},{5,4},{6,5},{7,6},{9,8},{10,9},{11,10},{12... | collective-permute-start | bytes 1928 | tf_op jit(solution)/shard_map/ppermute | solution.py:26
  279.2 11.7 %broadcast_in_dim.2 = f32[3,8,8,8,32,8]{5,4,3,2,1,0:T(8,128)} broadcast(f32[3,8,32]{2,1,0:T(8,128)S(1)} %fusion.78), dimensions={0,2,4} | broadcast | bytes 1575936 | tf_op jit(solution)/shard_map/broadcast_in_dim | solution.py:109
  290.9 19.4 %reshape.24 = f32[24,64,256]{2,1,0:T(8,128)} reshape(f32[3,8,8,8,32,8]{5,4,3,2,1,0:T(8,128)} %broadcast_in_dim.2) | data formatting | bytes 3145728 | tf_op jit(solution)/shard_map/reshape | solution.py:113
  310.3 3.1 fusion.137
  313.4 2.9 collective-permute-start.37
  318.2 5.8 %collective-permute-done.36 = f32[1,64,256]{2,1,0:T(8,128)S(1)} collective-permute-done((f32[1,64,256]{2,1,0:T(8,128)S(1)}, f32[1,64,256]{2,1,0:T(8,128)S(1)}, u32[]{:S(2)}, u32[]{:S(2)}) %collective-permute-start.36) | collective-permute-done | bytes 65568 | tf_op jit(solution)/shard_map/ppermute | solution.py:26
  324.0 5.1 %collective-permute-start.38 = (f32[26,1,256]{2,1,0:T(1,128)S(1)}, f32[26,1,256]{2,1,0:T(1,128)S(1)}, u32[]{:S(2)}, u32[]{:S(2)}) collective-permute-start(f32[26,1,256]{2,1,0:T(1,128)S(1)} %get-tuple-element.20), channel_id=1, source_target_pairs={{1,0},{2,1},{3,2},{4,3},{5,4},{6,5},{7,6},{9,8},{10,9},{11,10},{12... | collective-permute-start | bytes 79880 | tf_op jit(solution)/shard_map/ppermute | solution.py:26
  331.1 3.9 %collective-permute-done.39 = f32[26,1,256]{2,1,0:T(1,128)S(1)} collective-permute-done((f32[26,1,256]{2,1,0:T(1,128)S(1)}, f32[26,1,256]{2,1,0:T(1,128)S(1)}, u32[]{:S(2)}, u32[]{:S(2)}) %collective-permute-start.39) | collective-permute-done | bytes 26656 | tf_op jit(solution)/shard_map/ppermute | solution.py:24
  335.0 3.4 fusion.141
  338.5 3.3 collective-permute-start.41
  343.7 5.8 %collective-permute-done.40 = f32[1,64,256]{2,1,0:T(8,128)S(1)} collective-permute-done((f32[1,64,256]{2,1,0:T(8,128)S(1)}, f32[1,64,256]{2,1,0:T(8,128)S(1)}, u32[]{:S(2)}, u32[]{:S(2)}) %collective-permute-start.40) | collective-permute-done | bytes 65568 | tf_op jit(solution)/shard_map/ppermute | solution.py:26
  351.4 3.6 collective-permute-start.43
  355.0 2.2 collective-permute-done.43
  357.2 3.1 fusion.139
  360.3 3.0 collective-permute-start.45
  365.3 5.8 %collective-permute-done.44 = f32[1,64,256]{2,1,0:T(8,128)S(1)} collective-permute-done((f32[1,64,256]{2,1,0:T(8,128)S(1)}, f32[1,64,256]{2,1,0:T(8,128)S(1)}, u32[]{:S(2)}, u32[]{:S(2)}) %collective-permute-start.44) | collective-permute-done | bytes 65568 | tf_op jit(solution)/shard_map/ppermute | solution.py:26
  373.0 3.4 collective-permute-start.47
  376.4 2.4 collective-permute-done.47
  378.8 3.9 %fusion.50 = f32[24,64,256]{2,1,0:T(8,128)} fusion(f32[24,64,256]{2,1,0:T(8,128)S(1)} %get-tuple-element.6, f32[24,64,256]{2,1,0:T(8,128)S(1)} %multiply_sqrt_fusion, f32[24,64,256]{2,1,0:T(8,128)S(1)} %get-tuple-element.5, f32[26,1,256]{2,1,0:T(1,128)S(1)} %collective-permute-done.47, f32[1,64,256]{2,1,0:T(8,128)S(1)} %collective-permute-done.44, ...), kind=kLoop, calls=%fused_computation.78 | loop fusion | flops 8257536 | bytes 9621504 | tf_op jit(solution)/shard_map/add | solution.py:144
  (140 shorter events, 58.0 us)
Async XLA Ops:
  2.4 5.6 %collective-permute-start.1 = (f32[1,64,256]{2,1,0:T(8,128)S(1)}, f32[1,64,256]{2,1,0:T(8,128)S(1)}, u32[]{:S(2)}, u32[]{:S(2)}) collective-permute-start(f32[1,64,256]{2,1,0:T(8,128)S(1)} %get-tuple-element.44), channel_id=1, source_target_pairs={{0,8},{8,16},{16,24},{24,32},{32,40},{40,48},{48,56},{56,64},{64,7... | collective-permute-start | bytes 196616 | tf_op jit(solution)/shard_map/ppermute | solution.py:24
  6.1 7.7 %collective-permute-start = (f32[1,64,256]{2,1,0:T(8,128)S(1)}, f32[1,64,256]{2,1,0:T(8,128)S(1)}, u32[]{:S(2)}, u32[]{:S(2)}) collective-permute-start(f32[1,64,256]{2,1,0:T(8,128)S(1)} %get-tuple-element.45), channel_id=1, source_target_pairs={{8,0},{16,8},{24,16},{32,24},{40,32},{48,40},{56,48},{64,56},{72,6... | collective-permute-start | bytes 196616 | tf_op jit(solution)/shard_map/ppermute | solution.py:26
  13.8 5.6 %collective-permute-start.2 = (f32[26,1,256]{2,1,0:T(1,128)S(1)}, f32[26,1,256]{2,1,0:T(1,128)S(1)}, u32[]{:S(2)}, u32[]{:S(2)}) collective-permute-start(f32[26,1,256]{2,1,0:T(1,128)S(1)} %get-tuple-element.30), channel_id=1, source_target_pairs={{1,0},{2,1},{3,2},{4,3},{5,4},{6,5},{7,6},{9,8},{10,9},{11,10},{12... | collective-permute-start | bytes 79880 | tf_op jit(solution)/shard_map/ppermute | solution.py:26
  15.8 6.5 %copy-start.3 = (s32[24,64,256]{2,1,0:T(8,128)S(1)}, s32[24,64,256]{2,1,0:T(8,128)}, u32[]{:S(2)}) copy-start(s32[24,64,256]{2,1,0:T(8,128)} %param.5) | copy-start | bytes 4718596
  15.8 6.5 %copy-start.14 = (f32[24,64,256]{2,1,0:T(8,128)S(1)}, f32[24,64,256]{2,1,0:T(8,128)}, u32[]{:S(2)}) copy-start(f32[24,64,256]{2,1,0:T(8,128)} %param.3) | copy-start | bytes 4718596
  15.8 6.1 %collective-permute-start.3 = (f32[26,1,256]{2,1,0:T(1,128)S(1)}, f32[26,1,256]{2,1,0:T(1,128)S(1)}, u32[]{:S(2)}, u32[]{:S(2)}) collective-permute-start(f32[26,1,256]{2,1,0:T(1,128)S(1)} %get-tuple-element.31), channel_id=1, source_target_pairs={{0,1},{1,2},{2,3},{3,4},{4,5},{5,6},{6,7},{8,9},{9,10},{10,11},{11... | collective-permute-start | bytes 79880 | tf_op jit(solution)/shard_map/ppermute | solution.py:24
  24.1 18.6 %copy-start = (f32[24,64,256]{2,1,0:T(8,128)}, f32[24,64,256]{2,1,0:T(8,128)S(1)}, u32[]{:S(2)}) copy-start(f32[24,64,256]{2,1,0:T(8,128)S(1)} %get-tuple-element.15) | copy-start | bytes 4718596
  24.1 18.6 %copy-start.5 = (f32[24,64,256]{2,1,0:T(8,128)}, f32[24,64,256]{2,1,0:T(8,128)S(1)}, u32[]{:S(2)}) copy-start(f32[24,64,256]{2,1,0:T(8,128)S(1)} %get-tuple-element.13) | copy-start | bytes 4718596
  24.2 5.1 %collective-permute-start.5 = (f32[1,64,256]{2,1,0:T(8,128)S(1)}, f32[1,64,256]{2,1,0:T(8,128)S(1)}, u32[]{:S(2)}, u32[]{:S(2)}) collective-permute-start(f32[1,64,256]{2,1,0:T(8,128)S(1)} %get-tuple-element.42), channel_id=1, source_target_pairs={{0,8},{8,16},{16,24},{24,32},{32,40},{40,48},{48,56},{56,64},{64,7... | collective-permute-start | bytes 196616 | tf_op jit(solution)/shard_map/ppermute | solution.py:24
  27.3 7.7 %collective-permute-start.4 = (f32[1,64,256]{2,1,0:T(8,128)S(1)}, f32[1,64,256]{2,1,0:T(8,128)S(1)}, u32[]{:S(2)}, u32[]{:S(2)}) collective-permute-start(f32[1,64,256]{2,1,0:T(8,128)S(1)} %get-tuple-element.43), channel_id=1, source_target_pairs={{8,0},{16,8},{24,16},{32,24},{40,32},{48,40},{56,48},{64,56},{72,6... | collective-permute-start | bytes 196616 | tf_op jit(solution)/shard_map/ppermute | solution.py:26
  35.0 6.6 %collective-permute-start.6 = (f32[26,1,256]{2,1,0:T(1,128)S(1)}, f32[26,1,256]{2,1,0:T(1,128)S(1)}, u32[]{:S(2)}, u32[]{:S(2)}) collective-permute-start(f32[26,1,256]{2,1,0:T(1,128)S(1)} %get-tuple-element.26), channel_id=1, source_target_pairs={{1,0},{2,1},{3,2},{4,3},{5,4},{6,5},{7,6},{9,8},{10,9},{11,10},{12... | collective-permute-start | bytes 79880 | tf_op jit(solution)/shard_map/ppermute | solution.py:26
  36.9 5.8 %collective-permute-start.7 = (f32[26,1,256]{2,1,0:T(1,128)S(1)}, f32[26,1,256]{2,1,0:T(1,128)S(1)}, u32[]{:S(2)}, u32[]{:S(2)}) collective-permute-start(f32[26,1,256]{2,1,0:T(1,128)S(1)} %get-tuple-element.27), channel_id=1, source_target_pairs={{0,1},{1,2},{2,3},{3,4},{4,5},{5,6},{6,7},{8,9},{9,10},{10,11},{11... | collective-permute-start | bytes 79880 | tf_op jit(solution)/shard_map/ppermute | solution.py:24
  41.6 4.2 %copy-start.19 = (f32[26,1,256]{2,1,0:T(1,128)}, f32[26,1,256]{2,1,0:T(1,128)S(1)}, u32[]{:S(2)}) copy-start(f32[26,1,256]{2,1,0:T(1,128)S(1)} %collective-permute-done.6) | copy-start | bytes 79876
  42.7 3.1 copy-start.21
  47.7 44.2 %collective-permute-start.9 = (f32[1,64,256]{2,1,0:T(8,128)}, f32[1,64,256]{2,1,0:T(8,128)S(1)}, u32[]{:S(2)}, u32[]{:S(2)}) collective-permute-start(f32[1,64,256]{2,1,0:T(8,128)} %get-tuple-element.40), channel_id=1, source_target_pairs={{0,8},{8,16},{16,24},{24,32},{32,40},{40,48},{48,56},{56,64},{64,7... | collective-permute-start | bytes 196616 | tf_op jit(solution)/shard_map/ppermute | solution.py:24
  50.7 41.2 %collective-permute-start.8 = (f32[1,64,256]{2,1,0:T(8,128)}, f32[1,64,256]{2,1,0:T(8,128)S(1)}, u32[]{:S(2)}, u32[]{:S(2)}) collective-permute-start(f32[1,64,256]{2,1,0:T(8,128)} %get-tuple-element.41), channel_id=1, source_target_pairs={{8,0},{16,8},{24,16},{32,24},{40,32},{48,40},{56,48},{64,56},{72,6... | collective-permute-start | bytes 196616 | tf_op jit(solution)/shard_map/ppermute | solution.py:26
  91.8 7.0 %copy-start.15 = (f32[1,64,256]{2,1,0:T(8,128)}, f32[1,64,256]{2,1,0:T(8,128)S(1)}, u32[]{:S(2)}) copy-start(f32[1,64,256]{2,1,0:T(8,128)S(1)} %collective-permute-done.9) | copy-start | bytes 196612
  91.8 7.0 %copy-start.17 = (f32[1,64,256]{2,1,0:T(8,128)}, f32[1,64,256]{2,1,0:T(8,128)S(1)}, u32[]{:S(2)}) copy-start(f32[1,64,256]{2,1,0:T(8,128)S(1)} %collective-permute-done.8) | copy-start | bytes 196612
  93.6 11.8 %collective-permute-start.10 = (f32[26,1,256]{2,1,0:T(1,128)}, f32[26,1,256]{2,1,0:T(1,128)}, u32[]{:S(2)}, u32[]{:S(2)}) collective-permute-start(f32[26,1,256]{2,1,0:T(1,128)} %get-tuple-element.24), channel_id=1, source_target_pairs={{1,0},{2,1},{3,2},{4,3},{5,4},{6,5},{7,6},{9,8},{10,9},{11,10},{12... | collective-permute-start | bytes 79880 | tf_op jit(solution)/shard_map/ppermute | solution.py:26
  95.5 9.9 %collective-permute-start.11 = (f32[26,1,256]{2,1,0:T(1,128)}, f32[26,1,256]{2,1,0:T(1,128)}, u32[]{:S(2)}, u32[]{:S(2)}) collective-permute-start(f32[26,1,256]{2,1,0:T(1,128)} %get-tuple-element.25), channel_id=1, source_target_pairs={{0,1},{1,2},{2,3},{3,4},{4,5},{5,6},{6,7},{8,9},{9,10},{10,11},{11... | collective-permute-start | bytes 79880 | tf_op jit(solution)/shard_map/ppermute | solution.py:24
  105.4 24.3 %copy-start.10 = (f32[26,65,256]{2,1,0:T(8,128)S(1)}, f32[26,65,256]{2,1,0:T(8,128)}, u32[]{:S(2)}) copy-start(f32[26,65,256]{2,1,0:T(8,128)} %copy-done.9) | copy-start | bytes 5191684
  105.4 24.3 %copy-start.12 = (f32[26,65,256]{2,1,0:T(8,128)S(1)}, f32[26,65,256]{2,1,0:T(8,128)}, u32[]{:S(2)}) copy-start(f32[26,65,256]{2,1,0:T(8,128)} %copy-done.11) | copy-start | bytes 5191684
  121.2 20.4 %collective-permute-start.13 = (f32[1,64,256]{2,1,0:T(8,128)}, f32[1,64,256]{2,1,0:T(8,128)S(1)}, u32[]{:S(2)}, u32[]{:S(2)}) collective-permute-start(f32[1,64,256]{2,1,0:T(8,128)} %get-tuple-element.38), channel_id=1, source_target_pairs={{0,8},{8,16},{16,24},{24,32},{32,40},{40,48},{48,56},{56,64},{64,7... | collective-permute-start | bytes 196616 | tf_op jit(solution)/shard_map/ppermute | solution.py:24
  127.5 14.1 %collective-permute-start.12 = (f32[1,64,256]{2,1,0:T(8,128)}, f32[1,64,256]{2,1,0:T(8,128)S(1)}, u32[]{:S(2)}, u32[]{:S(2)}) collective-permute-start(f32[1,64,256]{2,1,0:T(8,128)} %get-tuple-element.39), channel_id=1, source_target_pairs={{8,0},{16,8},{24,16},{32,24},{40,32},{48,40},{56,48},{64,56},{72,6... | collective-permute-start | bytes 196616 | tf_op jit(solution)/shard_map/ppermute | solution.py:26
  141.6 9.9 %copy-start.1 = (f32[24,64,256]{2,1,0:T(8,128)S(1)}, f32[24,64,256]{2,1,0:T(8,128)}, u32[]{:S(2)}) copy-start(f32[24,64,256]{2,1,0:T(8,128)} %copy-done) | copy-start | bytes 4718596
  142.8 5.3 %collective-permute-start.14 = (f32[26,1,256]{2,1,0:T(1,128)S(1)}, f32[26,1,256]{2,1,0:T(1,128)S(1)}, u32[]{:S(2)}, u32[]{:S(2)}) collective-permute-start(f32[26,1,256]{2,1,0:T(1,128)S(1)} %get-tuple-element.22), channel_id=1, source_target_pairs={{1,0},{2,1},{3,2},{4,3},{5,4},{6,5},{7,6},{9,8},{10,9},{11,10},{12... | collective-permute-start | bytes 79880 | tf_op jit(solution)/shard_map/ppermute | solution.py:26
  145.7 5.8 %collective-permute-start.15 = (f32[26,1,256]{2,1,0:T(1,128)S(1)}, f32[26,1,256]{2,1,0:T(1,128)S(1)}, u32[]{:S(2)}, u32[]{:S(2)}) collective-permute-start(f32[26,1,256]{2,1,0:T(1,128)S(1)} %get-tuple-element.23), channel_id=1, source_target_pairs={{0,1},{1,2},{2,3},{3,4},{4,5},{5,6},{6,7},{8,9},{9,10},{10,11},{11... | collective-permute-start | bytes 79880 | tf_op jit(solution)/shard_map/ppermute | solution.py:24
  176.9 9.5 %copy-start.23 = (f32[3,8,32]{2,1,0:T(8,128)S(1)}, f32[3,8,32]{2,1,0:T(8,128)}, u32[]{:S(2)}) copy-start(f32[3,8,32]{2,1,0:T(8,128)} %reduce_sum.46) | copy-start | bytes 9220
  186.5 9.1 %collective-permute-start.16 = (f32[1,8,32]{2,1,0:T(8,128)S(1)}, f32[1,8,32]{2,1,0:T(8,128)S(1)}, u32[]{:S(2)}, u32[]{:S(2)}) collective-permute-start(f32[1,8,32]{2,1,0:T(8,128)S(1)} %get-tuple-element.66), channel_id=1, source_target_pairs={{0,8},{8,16},{16,24},{24,32},{32,40},{40,48},{48,56},{56,64},{64,7... | collective-permute-start | bytes 3080 | tf_op jit(solution)/shard_map/ppermute | solution.py:24
  193.7 7.0 %collective-permute-start.17 = (f32[1,8,32]{2,1,0:T(8,128)S(1)}, f32[1,8,32]{2,1,0:T(8,128)S(1)}, u32[]{:S(2)}, u32[]{:S(2)}) collective-permute-start(f32[1,8,32]{2,1,0:T(8,128)S(1)} %get-tuple-element.67), channel_id=1, source_target_pairs={{8,0},{16,8},{24,16},{32,24},{40,32},{48,40},{56,48},{64,56},{72,6... | collective-permute-start | bytes 3080 | tf_op jit(solution)/shard_map/ppermute | solution.py:26
  200.8 6.5 %collective-permute-start.18 = (f32[5,1,32]{2,1,0:T(1,128)S(1)}, f32[5,1,32]{2,1,0:T(1,128)S(1)}, u32[]{:S(2)}, u32[]{:S(2)}) collective-permute-start(f32[5,1,32]{2,1,0:T(1,128)S(1)} %get-tuple-element.54), channel_id=1, source_target_pairs={{0,1},{1,2},{2,3},{3,4},{4,5},{5,6},{6,7},{8,9},{9,10},{10,11},{11... | collective-permute-start | bytes 1928 | tf_op jit(solution)/shard_map/ppermute | solution.py:24
  202.7 5.3 %collective-permute-start.19 = (f32[5,1,32]{2,1,0:T(1,128)S(1)}, f32[5,1,32]{2,1,0:T(1,128)S(1)}, u32[]{:S(2)}, u32[]{:S(2)}) collective-permute-start(f32[5,1,32]{2,1,0:T(1,128)S(1)} %get-tuple-element.55), channel_id=1, source_target_pairs={{1,0},{2,1},{3,2},{4,3},{5,4},{6,5},{7,6},{9,8},{10,9},{11,10},{12... | collective-permute-start | bytes 1928 | tf_op jit(solution)/shard_map/ppermute | solution.py:26
  208.1 5.0 %collective-permute-start.20 = (f32[1,8,32]{2,1,0:T(8,128)S(1)}, f32[1,8,32]{2,1,0:T(8,128)S(1)}, u32[]{:S(2)}, u32[]{:S(2)}) collective-permute-start(f32[1,8,32]{2,1,0:T(8,128)S(1)} %get-tuple-element.64), channel_id=1, source_target_pairs={{0,8},{8,16},{16,24},{24,32},{32,40},{40,48},{48,56},{56,64},{64,7... | collective-permute-start | bytes 3080 | tf_op jit(solution)/shard_map/ppermute | solution.py:24
  211.2 7.0 %collective-permute-start.21 = (f32[1,8,32]{2,1,0:T(8,128)S(1)}, f32[1,8,32]{2,1,0:T(8,128)S(1)}, u32[]{:S(2)}, u32[]{:S(2)}) collective-permute-start(f32[1,8,32]{2,1,0:T(8,128)S(1)} %get-tuple-element.65), channel_id=1, source_target_pairs={{8,0},{16,8},{24,16},{32,24},{40,32},{48,40},{56,48},{64,56},{72,6... | collective-permute-start | bytes 3080 | tf_op jit(solution)/shard_map/ppermute | solution.py:26
  218.2 7.1 %collective-permute-start.22 = (f32[5,1,32]{2,1,0:T(1,128)S(1)}, f32[5,1,32]{2,1,0:T(1,128)S(1)}, u32[]{:S(2)}, u32[]{:S(2)}) collective-permute-start(f32[5,1,32]{2,1,0:T(1,128)S(1)} %get-tuple-element.52), channel_id=1, source_target_pairs={{0,1},{1,2},{2,3},{3,4},{4,5},{5,6},{6,7},{8,9},{9,10},{10,11},{11... | collective-permute-start | bytes 1928 | tf_op jit(solution)/shard_map/ppermute | solution.py:24
  220.1 5.8 %collective-permute-start.23 = (f32[5,1,32]{2,1,0:T(1,128)S(1)}, f32[5,1,32]{2,1,0:T(1,128)S(1)}, u32[]{:S(2)}, u32[]{:S(2)}) collective-permute-start(f32[5,1,32]{2,1,0:T(1,128)S(1)} %get-tuple-element.53), channel_id=1, source_target_pairs={{1,0},{2,1},{3,2},{4,3},{5,4},{6,5},{7,6},{9,8},{10,9},{11,10},{12... | collective-permute-start | bytes 1928 | tf_op jit(solution)/shard_map/ppermute | solution.py:26
  226.1 4.7 %collective-permute-start.24 = (f32[1,8,32]{2,1,0:T(8,128)S(1)}, f32[1,8,32]{2,1,0:T(8,128)S(1)}, u32[]{:S(2)}, u32[]{:S(2)}) collective-permute-start(f32[1,8,32]{2,1,0:T(8,128)S(1)} %get-tuple-element.62), channel_id=1, source_target_pairs={{0,8},{8,16},{16,24},{24,32},{32,40},{40,48},{48,56},{56,64},{64,7... | collective-permute-start | bytes 3080 | tf_op jit(solution)/shard_map/ppermute | solution.py:24
  228.9 7.0 %collective-permute-start.25 = (f32[1,8,32]{2,1,0:T(8,128)S(1)}, f32[1,8,32]{2,1,0:T(8,128)S(1)}, u32[]{:S(2)}, u32[]{:S(2)}) collective-permute-start(f32[1,8,32]{2,1,0:T(8,128)S(1)} %get-tuple-element.63), channel_id=1, source_target_pairs={{8,0},{16,8},{24,16},{32,24},{40,32},{48,40},{56,48},{64,56},{72,6... | collective-permute-start | bytes 3080 | tf_op jit(solution)/shard_map/ppermute | solution.py:26
  235.9 7.1 %collective-permute-start.26 = (f32[5,1,32]{2,1,0:T(1,128)S(1)}, f32[5,1,32]{2,1,0:T(1,128)S(1)}, u32[]{:S(2)}, u32[]{:S(2)}) collective-permute-start(f32[5,1,32]{2,1,0:T(1,128)S(1)} %get-tuple-element.50), channel_id=1, source_target_pairs={{0,1},{1,2},{2,3},{3,4},{4,5},{5,6},{6,7},{8,9},{9,10},{10,11},{11... | collective-permute-start | bytes 1928 | tf_op jit(solution)/shard_map/ppermute | solution.py:24
  237.9 5.8 %collective-permute-start.27 = (f32[5,1,32]{2,1,0:T(1,128)S(1)}, f32[5,1,32]{2,1,0:T(1,128)S(1)}, u32[]{:S(2)}, u32[]{:S(2)}) collective-permute-start(f32[5,1,32]{2,1,0:T(1,128)S(1)} %get-tuple-element.51), channel_id=1, source_target_pairs={{1,0},{2,1},{3,2},{4,3},{5,4},{6,5},{7,6},{9,8},{10,9},{11,10},{12... | collective-permute-start | bytes 1928 | tf_op jit(solution)/shard_map/ppermute | solution.py:26
  243.8 4.7 %collective-permute-start.28 = (f32[1,8,32]{2,1,0:T(8,128)S(1)}, f32[1,8,32]{2,1,0:T(8,128)S(1)}, u32[]{:S(2)}, u32[]{:S(2)}) collective-permute-start(f32[1,8,32]{2,1,0:T(8,128)S(1)} %get-tuple-element.60), channel_id=1, source_target_pairs={{0,8},{8,16},{16,24},{24,32},{32,40},{40,48},{48,56},{56,64},{64,7... | collective-permute-start | bytes 3080 | tf_op jit(solution)/shard_map/ppermute | solution.py:24
  246.6 7.0 %collective-permute-start.29 = (f32[1,8,32]{2,1,0:T(8,128)S(1)}, f32[1,8,32]{2,1,0:T(8,128)S(1)}, u32[]{:S(2)}, u32[]{:S(2)}) collective-permute-start(f32[1,8,32]{2,1,0:T(8,128)S(1)} %get-tuple-element.61), channel_id=1, source_target_pairs={{8,0},{16,8},{24,16},{32,24},{40,32},{48,40},{56,48},{64,56},{72,6... | collective-permute-start | bytes 3080 | tf_op jit(solution)/shard_map/ppermute | solution.py:26
  253.6 7.1 %collective-permute-start.30 = (f32[5,1,32]{2,1,0:T(1,128)S(1)}, f32[5,1,32]{2,1,0:T(1,128)S(1)}, u32[]{:S(2)}, u32[]{:S(2)}) collective-permute-start(f32[5,1,32]{2,1,0:T(1,128)S(1)} %get-tuple-element.48), channel_id=1, source_target_pairs={{0,1},{1,2},{2,3},{3,4},{4,5},{5,6},{6,7},{8,9},{9,10},{10,11},{11... | collective-permute-start | bytes 1928 | tf_op jit(solution)/shard_map/ppermute | solution.py:24
  255.6 5.8 %collective-permute-start.31 = (f32[5,1,32]{2,1,0:T(1,128)S(1)}, f32[5,1,32]{2,1,0:T(1,128)S(1)}, u32[]{:S(2)}, u32[]{:S(2)}) collective-permute-start(f32[5,1,32]{2,1,0:T(1,128)S(1)} %get-tuple-element.49), channel_id=1, source_target_pairs={{1,0},{2,1},{3,2},{4,3},{5,4},{6,5},{7,6},{9,8},{10,9},{11,10},{12... | collective-permute-start | bytes 1928 | tf_op jit(solution)/shard_map/ppermute | solution.py:26
  261.5 4.7 %collective-permute-start.32 = (f32[1,8,32]{2,1,0:T(8,128)S(1)}, f32[1,8,32]{2,1,0:T(8,128)S(1)}, u32[]{:S(2)}, u32[]{:S(2)}) collective-permute-start(f32[1,8,32]{2,1,0:T(8,128)S(1)} %get-tuple-element.58), channel_id=1, source_target_pairs={{0,8},{8,16},{16,24},{24,32},{32,40},{40,48},{48,56},{56,64},{64,7... | collective-permute-start | bytes 3080 | tf_op jit(solution)/shard_map/ppermute | solution.py:24
  264.3 7.0 %collective-permute-start.33 = (f32[1,8,32]{2,1,0:T(8,128)S(1)}, f32[1,8,32]{2,1,0:T(8,128)S(1)}, u32[]{:S(2)}, u32[]{:S(2)}) collective-permute-start(f32[1,8,32]{2,1,0:T(8,128)S(1)} %get-tuple-element.59), channel_id=1, source_target_pairs={{8,0},{16,8},{24,16},{32,24},{40,32},{48,40},{56,48},{64,56},{72,6... | collective-permute-start | bytes 3080 | tf_op jit(solution)/shard_map/ppermute | solution.py:26
  271.4 7.1 %collective-permute-start.34 = (f32[5,1,32]{2,1,0:T(1,128)S(1)}, f32[5,1,32]{2,1,0:T(1,128)S(1)}, u32[]{:S(2)}, u32[]{:S(2)}) collective-permute-start(f32[5,1,32]{2,1,0:T(1,128)S(1)} %get-tuple-element.46), channel_id=1, source_target_pairs={{0,1},{1,2},{2,3},{3,4},{4,5},{5,6},{6,7},{8,9},{9,10},{10,11},{11... | collective-permute-start | bytes 1928 | tf_op jit(solution)/shard_map/ppermute | solution.py:24
  273.3 5.8 %collective-permute-start.35 = (f32[5,1,32]{2,1,0:T(1,128)S(1)}, f32[5,1,32]{2,1,0:T(1,128)S(1)}, u32[]{:S(2)}, u32[]{:S(2)}) collective-permute-start(f32[5,1,32]{2,1,0:T(1,128)S(1)} %get-tuple-element.47), channel_id=1, source_target_pairs={{1,0},{2,1},{3,2},{4,3},{5,4},{6,5},{7,6},{9,8},{10,9},{11,10},{12... | collective-permute-start | bytes 1928 | tf_op jit(solution)/shard_map/ppermute | solution.py:26
  310.2 24.7 %copy-start.4 = (s32[24,64,256]{2,1,0:T(8,128)S(1)}, s32[24,64,256]{2,1,0:T(8,128)}, u32[]{:S(2)}) copy-start(s32[24,64,256]{2,1,0:T(8,128)} %param.5) | copy-start | bytes 4718596
  310.2 24.7 %copy-start.6 = (f32[24,64,256]{2,1,0:T(8,128)S(1)}, f32[24,64,256]{2,1,0:T(8,128)}, u32[]{:S(2)}) copy-start(f32[24,64,256]{2,1,0:T(8,128)} %get-tuple-element.12) | copy-start | bytes 4718596
  310.3 24.7 %copy-start.13 = (f32[24,64,256]{2,1,0:T(8,128)S(1)}, f32[24,64,256]{2,1,0:T(8,128)}, u32[]{:S(2)}) copy-start(f32[24,64,256]{2,1,0:T(8,128)} %reshape.24) | copy-start | bytes 4718596
  313.3 21.6 %copy-start.2 = (f32[24,64,256]{2,1,0:T(8,128)S(1)}, f32[24,64,256]{2,1,0:T(8,128)}, u32[]{:S(2)}) copy-start(f32[24,64,256]{2,1,0:T(8,128)} %copy-done) | copy-start | bytes 4718596
  313.4 4.9 %collective-permute-start.37 = (f32[1,64,256]{2,1,0:T(8,128)S(1)}, f32[1,64,256]{2,1,0:T(8,128)S(1)}, u32[]{:S(2)}, u32[]{:S(2)}) collective-permute-start(f32[1,64,256]{2,1,0:T(8,128)S(1)} %get-tuple-element.36), channel_id=1, source_target_pairs={{0,8},{8,16},{16,24},{24,32},{32,40},{40,48},{48,56},{56,64},{64,7... | collective-permute-start | bytes 196616 | tf_op jit(solution)/shard_map/ppermute | solution.py:24
  316.3 7.7 %collective-permute-start.36 = (f32[1,64,256]{2,1,0:T(8,128)S(1)}, f32[1,64,256]{2,1,0:T(8,128)S(1)}, u32[]{:S(2)}, u32[]{:S(2)}) collective-permute-start(f32[1,64,256]{2,1,0:T(8,128)S(1)} %get-tuple-element.37), channel_id=1, source_target_pairs={{8,0},{16,8},{24,16},{32,24},{40,32},{48,40},{56,48},{64,56},{72,6... | collective-permute-start | bytes 196616 | tf_op jit(solution)/shard_map/ppermute | solution.py:26
  324.0 7.1 %collective-permute-start.38 = (f32[26,1,256]{2,1,0:T(1,128)S(1)}, f32[26,1,256]{2,1,0:T(1,128)S(1)}, u32[]{:S(2)}, u32[]{:S(2)}) collective-permute-start(f32[26,1,256]{2,1,0:T(1,128)S(1)} %get-tuple-element.20), channel_id=1, source_target_pairs={{1,0},{2,1},{3,2},{4,3},{5,4},{6,5},{7,6},{9,8},{10,9},{11,10},{12... | collective-permute-start | bytes 79880 | tf_op jit(solution)/shard_map/ppermute | solution.py:26
  329.2 5.8 %collective-permute-start.39 = (f32[26,1,256]{2,1,0:T(1,128)S(1)}, f32[26,1,256]{2,1,0:T(1,128)S(1)}, u32[]{:S(2)}, u32[]{:S(2)}) collective-permute-start(f32[26,1,256]{2,1,0:T(1,128)S(1)} %get-tuple-element.21), channel_id=1, source_target_pairs={{0,1},{1,2},{2,3},{3,4},{4,5},{5,6},{6,7},{8,9},{9,10},{10,11},{11... | collective-permute-start | bytes 79880 | tf_op jit(solution)/shard_map/ppermute | solution.py:24
  338.5 5.2 %collective-permute-start.41 = (f32[1,64,256]{2,1,0:T(8,128)S(1)}, f32[1,64,256]{2,1,0:T(8,128)S(1)}, u32[]{:S(2)}, u32[]{:S(2)}) collective-permute-start(f32[1,64,256]{2,1,0:T(8,128)S(1)} %get-tuple-element.34), channel_id=1, source_target_pairs={{0,8},{8,16},{16,24},{24,32},{32,40},{40,48},{48,56},{56,64},{64,7... | collective-permute-start | bytes 196616 | tf_op jit(solution)/shard_map/ppermute | solution.py:24
  341.8 7.7 %collective-permute-start.40 = (f32[1,64,256]{2,1,0:T(8,128)S(1)}, f32[1,64,256]{2,1,0:T(8,128)S(1)}, u32[]{:S(2)}, u32[]{:S(2)}) collective-permute-start(f32[1,64,256]{2,1,0:T(8,128)S(1)} %get-tuple-element.35), channel_id=1, source_target_pairs={{8,0},{16,8},{24,16},{32,24},{40,32},{48,40},{56,48},{64,56},{72,6... | collective-permute-start | bytes 196616 | tf_op jit(solution)/shard_map/ppermute | solution.py:26
  349.5 5.5 %collective-permute-start.42 = (f32[26,1,256]{2,1,0:T(1,128)S(1)}, f32[26,1,256]{2,1,0:T(1,128)S(1)}, u32[]{:S(2)}, u32[]{:S(2)}) collective-permute-start(f32[26,1,256]{2,1,0:T(1,128)S(1)} %get-tuple-element.18), channel_id=1, source_target_pairs={{1,0},{2,1},{3,2},{4,3},{5,4},{6,5},{7,6},{9,8},{10,9},{11,10},{12... | collective-permute-start | bytes 79880 | tf_op jit(solution)/shard_map/ppermute | solution.py:26
  351.4 5.8 %collective-permute-start.43 = (f32[26,1,256]{2,1,0:T(1,128)S(1)}, f32[26,1,256]{2,1,0:T(1,128)S(1)}, u32[]{:S(2)}, u32[]{:S(2)}) collective-permute-start(f32[26,1,256]{2,1,0:T(1,128)S(1)} %get-tuple-element.19), channel_id=1, source_target_pairs={{0,1},{1,2},{2,3},{3,4},{4,5},{5,6},{6,7},{8,9},{9,10},{10,11},{11... | collective-permute-start | bytes 79880 | tf_op jit(solution)/shard_map/ppermute | solution.py:24
  360.3 5.0 %collective-permute-start.45 = (f32[1,64,256]{2,1,0:T(8,128)S(1)}, f32[1,64,256]{2,1,0:T(8,128)S(1)}, u32[]{:S(2)}, u32[]{:S(2)}) collective-permute-start(f32[1,64,256]{2,1,0:T(8,128)S(1)} %get-tuple-element.32), channel_id=1, source_target_pairs={{0,8},{8,16},{16,24},{24,32},{32,40},{40,48},{48,56},{56,64},{64,7... | collective-permute-start | bytes 196616 | tf_op jit(solution)/shard_map/ppermute | solution.py:24
  363.4 7.7 %collective-permute-start.44 = (f32[1,64,256]{2,1,0:T(8,128)S(1)}, f32[1,64,256]{2,1,0:T(8,128)S(1)}, u32[]{:S(2)}, u32[]{:S(2)}) collective-permute-start(f32[1,64,256]{2,1,0:T(8,128)S(1)} %get-tuple-element.33), channel_id=1, source_target_pairs={{8,0},{16,8},{24,16},{32,24},{40,32},{48,40},{56,48},{64,56},{72,6... | collective-permute-start | bytes 196616 | tf_op jit(solution)/shard_map/ppermute | solution.py:26
  371.1 5.3 %collective-permute-start.46 = (f32[26,1,256]{2,1,0:T(1,128)S(1)}, f32[26,1,256]{2,1,0:T(1,128)S(1)}, u32[]{:S(2)}, u32[]{:S(2)}) collective-permute-start(f32[26,1,256]{2,1,0:T(1,128)S(1)} %get-tuple-element.16), channel_id=1, source_target_pairs={{1,0},{2,1},{3,2},{4,3},{5,4},{6,5},{7,6},{9,8},{10,9},{11,10},{12... | collective-permute-start | bytes 79880 | tf_op jit(solution)/shard_map/ppermute | solution.py:26
  373.0 5.8 %collective-permute-start.47 = (f32[26,1,256]{2,1,0:T(1,128)S(1)}, f32[26,1,256]{2,1,0:T(1,128)S(1)}, u32[]{:S(2)}, u32[]{:S(2)}) collective-permute-start(f32[26,1,256]{2,1,0:T(1,128)S(1)} %get-tuple-element.17), channel_id=1, source_target_pairs={{0,1},{1,2},{2,3},{3,4},{4,5},{5,6},{6,7},{8,9},{9,10},{10,11},{11... | collective-permute-start | bytes 79880 | tf_op jit(solution)/shard_map/ppermute | solution.py:24
  (8 other events, 16.6 us)
where the time goes:
time: 385 us; the launch traced here: 383 us
  starting transfers between devices  141 us (37%)
  local copies, waits for them, and re-layouts  90 us (23%)
  other arithmetic  77.4 us (20%)
  waiting for transfers between devices  73.3 us (19%)
    ppermute x24, starting transfers between devices, padded_2(): lax.ppermute(tail, axis, [(i, (i + 1) % count) for i in range(ends)])  75.2 us
    ppermute x24, starting transfers between devices, padded_2(): lax.ppermute(head, axis, [((i + 1) % count, i) for i in range(ends)])  65.8 us
    ppermute x24, waiting for transfers between devices, padded_2(): lax.ppermute(head, axis, [((i + 1) % count, i) for i in range(ends)])  57.8 us
    reshape x2, local copies, waits for them, and re-layouts, aggregate(): values.reshape(dims[0] // COARSEN, COARSEN, dims[1] // COARSEN, COARSEN,...  34.5 us
    mul x6, other arithmetic, coupling(): padded = padded_2(root_coef * iterate, (('region', 0), ('block', 1)), 1)  28.3 us
    reduce_sum x2, other arithmetic, aggregate(): return shaped.sum(axis=(1, 3, 5))  19.6 us
    reshape x1, local copies, waits for them, and re-layouts, prolong(): return wide.reshape(dims[0] * COARSEN, dims[1] * COARSEN, dims[2] * COARSEN)  19.4 us
    ppermute x24, waiting for transfers between devices, padded_2(): lax.ppermute(tail, axis, [(i, (i + 1) % count) for i in range(ends)])  15.4 us
  transfers between devices with their start and end apart: 48, of which 21 were waited for; matrix products, arithmetic and copies ran while one was open for 15% of the time, Pallas kernels for 0%

commit v1 on v0

v1 whole, which is shorter than its diff:
```python
import functools

import jax
import jax.numpy as jnp
from jax import lax
from jax.experimental import pallas as pl
from jax.experimental.pallas import tpu as pltpu
from jax.sharding import PartitionSpec as P

MESH = pl.DeviceIdType.MESH
F32 = jnp.float32
NREG, NBLK = 32, 8
XL = 24
YV = 9
XO = 3
MASS = 0.05
RELAX = 0.8

NEAR = [(dr, db) for dr in (-2, -1, 0, 1, 2) for db in (-1, 0, 1) if (dr, db) != (0, 0)]
FAR = [(dr, db) for dr in (-3, 3) for db in (-1, 0, 1)]
CORNERS = [(dr, db) for dr in (-1, 1) for db in (-1, 1)]


def iota(axis, shape=(8, 128)):
    return lax.broadcasted_iota(jnp.int32, shape, axis)


def z_sides(a, b):
    lane = iota(2, (1, 8, 128))
    first, last = lane == 0, lane == 127
    ra, rb = pltpu.roll(a, 1, 2), pltpu.roll(b, 1, 2)
    la, lb = pltpu.roll(a, 127, 2), pltpu.roll(b, 127, 2)
    low = (jnp.where(first, 0.0, ra), jnp.where(first, ra, rb))
    high = (jnp.where(last, lb, la), jnp.where(last, 0.0, lb))
    return low, high


def y_sides(a):
    down = jnp.concatenate([pltpu.roll(a[YV - 1 :], 1, 1), a[: YV - 1]], axis=0)
    up = jnp.concatenate([a[1:], pltpu.roll(a[:1], 7, 1)], axis=0)
    return down, up


def around(ref, X):
    a, b = ref[X, 0], ref[X, 1]
    low, high = z_sides(a, b)
    out = []
    for h, v in ((0, a), (1, b)):
        down, up = y_sides(v)
        out.append((low[h] + high[h]) + (down + up) + (ref[X - 1, h] + ref[X + 1, h]))
    return (a, b), out


def y_total(v):
    sub = iota(0)
    same, less, more = None, None, None
    for i in range(YV):
        lo, hi = 4 - i, 12 - i
        s = v[i]
        if i < 4:
            t = jnp.where((sub < lo) & (sub > 0), s, 0.0)
            less = t if less is None else less + t
            s = jnp.where(sub >= lo, s, 0.0)
        elif i > 4:
            t = jnp.where((sub >= hi) & (sub < 7), s, 0.0)
            more = t if more is None else more + t
            s = jnp.where(sub < hi, s, 0.0)
        same = s if same is None else same + s
    return same + pltpu.roll(less, 7, 0) + pltpu.roll(more, 1, 0)


def dot(a, b):
    return jnp.dot(a, b, precision=lax.Precision.HIGHEST, preferred_element_type=F32)


def kernel(
    k_ref, solid_ref, rs_ref, out_ref,
    kn, sn, cn, rn, cs, S, G, W, RC, UA, UB, on,
    ysend, yrecv, csend, crecv, usend, urecv, vsend, vrecv, xhalo,
    racc, tacc, cnt, czacc, cyacc, zacc, CM, RM, CO, RO, pz, px, po,
    load_sem, out_sem, ss, rr,
):
    r = lax.axis_index("region")
    b = lax.axis_index("block")

    def dev(dr, db):
        return (lax.rem(r + (dr + NREG), NREG), lax.rem(b + (db + NBLK), NBLK))

    bar = pltpu.get_barrier_semaphore()
    for off in NEAR + FAR:
        pl.semaphore_signal(bar, inc=1, device_id=dev(*off), device_id_type=MESH)

    loads = []
    for i, (src, dst) in enumerate(((k_ref, kn), (solid_ref, sn), (rs_ref, rn.at[2 : 2 + XL, :, 8:72, :]))):
        for h in range(2):
            cp = pltpu.make_async_copy(
                src.at[:, :, pl.ds(128 * h, 128)], dst.at[:, h], load_sem.at[2 * i + h]
            )
            cp.start()
            loads.append(cp)

    row, col = iota(0, (256, 128)), iota(1, (256, 128))
    cell = lax.rem(col, 32)
    pz[...] = jnp.where(lax.div(row, 8) == cell, 1.0, 0.0)
    po[...] = jnp.where(row == 8 * cell, 1.0, 0.0)
    row, col = iota(0, (128, 256)), iota(1, (128, 256))
    px[...] = jnp.where(row - 32 == lax.div(col, 8), 1.0, 0.0)
    zero8 = jnp.zeros((8, 128), F32)
    zeros9 = jnp.zeros((YV, 8, 128), F32)

    def clear(x, _):
        for h in range(2):
            cn[x, h, 0:8, :] = zero8
            cn[x, h, 72:80, :] = zero8
            rn[jnp.minimum(x, XL + 3), h, 0:8, :] = zero8
            rn[jnp.minimum(x, XL + 3), h, 72:80, :] = zero8
        return 0

    lax.fori_loop(0, XL + 2 * XO, clear, 0)
    for h in range(2):
        UB[XO - 1, h] = zeros9
        UB[XO + XL, h] = zeros9
        for s in range(3):
            for ref in (racc, cnt, czacc, cyacc):
                ref[s, h] = zeros9
            for ref in (tacc, zacc):
                ref[s, h] = zero8

    for cp in loads[:4]:
        cp.wait()

    def root(x, _):
        for h in range(2):
            k = kn[x, h]
            cn[x + XO, h, 8:72, :] = jnp.where(sn[x, h] == 0, k * lax.rsqrt(k), 0.0)
        return 0

    lax.fori_loop(0, XL, root, 0)
    for cp in loads[4:]:
        cp.wait()

    def pack(x, _):
        for h in range(2):
            for side in range(2):
                for j in range(3):
                    y = j if side == 0 else 61 + j
                    ysend[side, (x * 2 + h) * 3 + j] = cn[x + XO, h, 8 + y : 9 + y, :]
                for j in range(2):
                    y = j if side == 0 else 62 + j
                    ysend[side, 144 + (x * 2 + h) * 2 + j] = rn[x + 2, h, 8 + y : 9 + y, :]
        return 0

    lax.fori_loop(0, XL, pack, 0)
    for n, (dr, db) in enumerate(CORNERS):
        for p in range(2):
            x = p if dr < 0 else XL - 2 + p
            for h in range(2):
                for j in range(2):
                    y = j if db < 0 else 62 + j
                    csend[n, (p * 2 + h) * 2 + j] = cn[x + XO, h, 8 + y : 9 + y, :]
        x, y = 0 if dr < 0 else XL - 1, 0 if db < 0 else 63
        for h in range(2):
            csend[n, 8 + h] = rn[x + 2, h, 8 + y : 9 + y, :]

    pl.semaphore_wait(bar, len(NEAR) + len(FAR))

    count = [0]

    def remote(src, dst, off):
        n = count[0]
        count[0] += 1
        cp = pltpu.make_async_remote_copy(
            src_ref=src, dst_ref=dst, send_sem=ss.at[n], recv_sem=rr.at[n],
            device_id=dev(*off), device_id_type=MESH,
        )
        cp.start()
        return cp

    ymsg = [remote(ysend.at[0], yrecv.at[1], (0, -1)), remote(ysend.at[1], yrecv.at[0], (0, 1))]
    xmsg = [
        remote(cn.at[3:6, :, 8:72, :], cn.at[27:30, :, 8:72, :], (-1, 0)),
        remote(cn.at[24:27, :, 8:72, :], cn.at[0:3, :, 8:72, :], (1, 0)),
        remote(rn.at[2:4, :, 8:72, :], rn.at[26:28, :, 8:72, :], (-1, 0)),
        remote(rn.at[24:26, :, 8:72, :], rn.at[0:2, :, 8:72, :], (1, 0)),
    ]
    cmsg = [remote(csend.at[n], crecv.at[3 - n], off) for n, off in enumerate(CORNERS)]

    def strided(ref, X, h):
        return jnp.stack([ref[X, h, pl.ds(4 + i, 8, stride=9), :] for i in range(YV)], axis=0)

    def deal(x, _):
        X = x + XO
        c = [strided(cn, X, h) for h in range(2)]
        low, _high = z_sides(*c)
        slab = lax.div(x, 8)
        for h in range(2):
            cs[X, h] = c[h]
            cnt[slab, h] += jnp.where(c[h] > 0.0, 1.0, 0.0)
            czacc[slab, h] += c[h] * low[h]
            cyacc[slab, h] += c[h] * y_sides(c[h])[0]
        return 0

    lax.fori_loop(0, XL, deal, 0)

    for cp in ymsg:
        cp.wait()
    below = jnp.where(b > 0, 1.0, 0.0).astype(F32)
    above = jnp.where(b < NBLK - 1, 1.0, 0.0).astype(F32)
    left = jnp.where(r > 0, 1.0, 0.0).astype(F32)
    right = jnp.where(r < NREG - 1, 1.0, 0.0).astype(F32)

    def unpack(x, _):
        for h in range(2):
            at = (x * 2 + h) * 3
            for j in range(3):
                cs[x + XO, h, 1 + j, 0:1, :] = yrecv[0, at + j] * below
                cs[x + XO, h, 5 + j, 7:8, :] = yrecv[1, at + j] * above
            at = 144 + (x * 2 + h) * 2
            for j in range(2):
                rn[x + 2, h, 6 + j : 7 + j, :] = yrecv[0, at + j]
                rn[x + 2, h, 72 + j : 73 + j, :] = yrecv[1, at + j]
        return 0

    lax.fori_loop(0, XL, unpack, 0)
    sub = iota(0)

    def edge(v):
        return jnp.where(sub == 0, v[3], jnp.where(sub == 7, v[5], 0.0))

    def setup(X, own):
        c, near = around(cs, X)
        for h in range(2):
            d = MASS + c[h] * near[h]
            pore = c[h] > 0.0
            safe = jnp.where(pore, c[h], 1.0)
            both = 1.0 / (d * safe)
            g = RELAX * c[h] * (both * safe)
            G[X, h] = g * c[h]
            S[X, h] = g * strided(rn, X - 1, h)
            if own:
                rc = jnp.where(pore, both * d, 0.0)
                RC[X, h] = rc
                W[X, h] = (1.0 / RELAX) * d * rc
                zacc[lax.div(X - XO, 8), h] += edge(c[h]) * c[h][4]

    def sweep(src, X):
        u, near = around(src, X)
        return [0.2 * u[h] + (S[X, h] + G[X, h] * near[h]) for h in range(2)]

    def first(X):
        for h, v in enumerate(sweep(S, X)):
            UA[X, h] = v

    vec, subs = iota(0, (YV, 8, 128)), iota(1, (YV, 8, 128))
    place = subs * YV + vec
    inside = (place >= 4) & (place < 68)

    def second(X):
        for h, v in enumerate(sweep(UA, X)):
            UB[X, h] = jnp.where(inside, v, 0.0)

    def resid(X):
        u, near = around(UB, X)
        slab = lax.div(X - XO, 8)
        for h in range(2):
            racc[slab, h] += W[X, h] * (S[X, h] - RELAX * u[h] + G[X, h] * near[h])
            tacc[slab, h] += edge(cs[X, h]) * u[h][4]

    def run(fn, lo, hi):
        def body(X, _):
            fn(X)
            return 0

        lax.fori_loop(lo + XO, hi + XO, body, 0)

    own_setup = functools.partial(setup, own=True)
    halo_setup = functools.partial(setup, own=False)
    run(own_setup, 1, 23)
    run(first, 2, 22)
    run(second, 3, 21)
    run(resid, 4, 20)

    for cp in xmsg + cmsg:
        cp.wait()
    for X, side in ((0, left), (1, left), (2, left), (27, right), (28, right), (29, right)):
        for h in range(2):
            cs[X, h] = strided(cn, X, h) * side
    for n, (dr, db) in enumerate(CORNERS):
        side = (left if dr < 0 else right) * (below if db < 0 else above)
        for p in range(2):
            X = (1 + p) if dr < 0 else (27 + p)
            for h in range(2):
                for j in range(2):
                    v = crecv[n, (p * 2 + h) * 2 + j] * side
                    if db < 0:
                        cs[X, h, 2 + j, 0:1, :] = v
                    else:
                        cs[X, h, 5 + j, 7:8, :] = v
        X, y = (1 if dr < 0 else 26), (7 if db < 0 else 72)
        for h in range(2):
            rn[X, h, y : y + 1, :] = crecv[n, 8 + h]
    run(halo_setup, -2, 0)
    run(own_setup, 0, 1)
    run(own_setup, 23, 24)
    run(halo_setup, 24, 26)
    run(first, -1, 2)
    run(first, 22, 25)
    run(second, 0, 3)
    run(second, 21, 24)
    run(resid, 0, 4)
    run(resid, 20, 24)

    def halves(fn):
        return jnp.concatenate([fn(0), fn(1)], axis=1)

    parts = [halves(lambda h, s=s: y_total(racc[s, h])) for s in range(3)]
    parts += [halves(lambda h, s=s: tacc[s, h]) for s in range(3)]
    parts += [halves(lambda h: y_total(cs[2, h] * UB[3, h])), halves(lambda h: y_total(cs[27, h] * UB[26, h]))]
    tot = dot(jnp.concatenate(parts, axis=0), pz[...])
    tot = [tot[8 * i : 8 * i + 8] for i in range(8)]
    group = lax.div(iota(1), 32)
    faces = [tot[6], zero8, tot[7]]
    for s in range(3):
        RM[7 + s, 1] = jnp.where(
            group == 0, tot[s], jnp.where(group == 1, tot[3 + s], jnp.where(group == 2, faces[s], 0.0))
        )
    rmsg = [
        remote(RM.at[7:10, 1], RM.at[7 - 3 * dr : 10 - 3 * dr, 1 - db], (dr, db)) for dr, db in NEAR
    ]
    for dr, db in FAR:
        s, t = (9, 0) if dr > 0 else (7, 16)
        rmsg.append(remote(RM.at[s, 1], RM.at[t, 1 - db], (dr, db)))

    planes = [y_pair(cs, 2, 3), y_pair(cs, 10, 11), y_pair(cs, 18, 19), y_pair(cs, 26, 27)]
    parts = [halves(lambda h, s=s: y_total(cnt[s, h])) for s in range(3)]
    parts += [halves(lambda h, p=p: p[h]) for p in planes]
    turn = lax.rem(vec + subs, 8) == 4

    def y_face(s, h):
        return y_total(jnp.where(turn, cyacc[s, h], 0.0)) + jnp.where(sub == 0, zacc[s, h], 0.0)

    parts += [halves(lambda h, s=s: y_face(s, h)) for s in range(3)]
    parts += [halves(lambda h, s=s: zacc[s, h]) for s in range(3)]
    tot = dot(jnp.concatenate(parts, axis=0), pz[...])
    tot = [tot[8 * i : 8 * i + 8] for i in range(13)]
    tz = dot(jnp.concatenate([halves(lambda h, s=s: y_total(czacc[s, h])) for s in range(3)], axis=0), po[...])
    for s in range(3):
        cx, cx2, cy, cz = tot[3 + s], tot[4 + s], tot[7 + s], tz[8 * s : 8 * s + 8]
        cy2 = jnp.where(sub == 7, tot[10 + s], pltpu.roll(cy, 7, 0))
        diag = MASS * (tot[s] + 1.0) + cx + cx2 + cy + cy2 + cz + pltpu.roll(cz, 127, 1)
        CM[6 + s, 1] = jnp.where(
            group == 0, RELAX / diag, jnp.where(group == 1, cx, jnp.where(group == 2, cy, cz))
        )
    kmsg = [
        remote(CM.at[6:9, 1], CM.at[6 - 3 * dr : 9 - 3 * dr, 1 - db], (dr, db)) for dr, db in NEAR
    ]

    def upack(x, _):
        for h in range(2):
            for j in range(3):
                usend[0, (x * 2 + h) * 3 + j] = UB[x + XO, h, 4 + j, 0:1, :]
                usend[1, (x * 2 + h) * 3 + j] = UB[x + XO, h, 2 + j, 7:8, :]
        return 0

    lax.fori_loop(0, XL, upack, 0)
    for n, (dr, db) in enumerate(CORNERS):
        for p in range(2):
            X = XO + (p if dr < 0 else XL - 2 + p)
            for h in range(2):
                for j in range(2):
                    at = (p * 2 + h) * 2 + j
                    vsend[n, at] = UB[X, h, 4 + j, 0:1, :] if db < 0 else UB[X, h, 3 + j, 7:8, :]
    uymsg = [remote(usend.at[0], urecv.at[1], (0, -1)), remote(usend.at[1], urecv.at[0], (0, 1))]
    uxmsg = [remote(UB.at[3:6], xhalo.at[1], (-1, 0)), remote(UB.at[24:27], xhalo.at[0], (1, 0))]
    ucmsg = [remote(vsend.at[n], vrecv.at[3 - n], off) for n, off in enumerate(CORNERS)]

    def gather(msgs, g):
        out = jnp.where(group == 2, pltpu.roll(msgs[2], (2 - g) % 4 * 32, 1) if g != 2 else msgs[2], 0.0)
        out = jnp.where(group == 1, pltpu.roll(msgs[1], (1 - g) % 4 * 32, 1) if g != 1 else msgs[1], out)
        return jnp.where(group == 0, pltpu.roll(msgs[0], (-g) % 4 * 32, 1) if g != 0 else msgs[0], out)

    def down_y(v):
        t = pltpu.roll(v, 1, 0)
        return jnp.where(sub == 0, pltpu.roll(t, 32, 1), t)

    def up_y(v):
        t = pltpu.roll(v, 7, 0)
        return jnp.where(sub == 7, pltpu.roll(t, 96, 1), t)

    for cp in kmsg:
        cp.wait()

    def coarse(s, _):
        msgs = [CM[s, i] for i in range(3)]
        q = gather(msgs, 0)
        cx = gather(msgs, 1)
        cy = gather(msgs, 2)
        cz = gather(msgs, 3)
        after = gather([CM[jnp.minimum(s + 1, 14), i] for i in range(3)], 1)
        CO[s, 0] = q
        CO[s, 1] = q * cx
        CO[s, 2] = q * after
        CO[s, 3] = q * cy
        CO[s, 4] = q * up_y(cy)
        CO[s, 5] = q * cz
        CO[s, 6] = q * jnp.where(group < 3, pltpu.roll(cz, 127, 1), 0.0)
        return 0

    lax.fori_loop(0, 15, coarse, 0)

    for cp in uymsg + uxmsg + ucmsg:
        cp.wait()

    def uunpack(x, _):
        for h in range(2):
            for j in range(3):
                UB[x + XO, h, 1 + j, 0:1, :] = urecv[0, (x * 2 + h) * 3 + j] * below
                UB[x + XO, h, 5 + j, 7:8, :] = urecv[1, (x * 2 + h) * 3 + j] * above
        return 0

    lax.fori_loop(0, XL, uunpack, 0)
    for X, n, i, side in (
        (0, 0, 0, left), (1, 0, 1, left), (2, 0, 2, left),
        (27, 1, 0, right), (28, 1, 1, right), (29, 1, 2, right),
    ):
        for h in range(2):
            UB[X, h] = xhalo[n, i, h] * side
    for n, (dr, db) in enumerate(CORNERS):
        side = (left if dr < 0 else right) * (below if db < 0 else above)
        for p in range(2):
            X = (1 + p) if dr < 0 else (27 + p)
            for h in range(2):
                for j in range(2):
                    v = vrecv[n, (p * 2 + h) * 2 + j] * side
                    if db < 0:
                        UB[X, h, 2 + j, 0:1, :] = v
                    else:
                        UB[X, h, 5 + j, 7:8, :] = v

    for cp in rmsg:
        cp.wait()

    def rhs(s):
        msgs = [RM[s + 1, i] for i in range(3)]
        res = gather(msgs, 0)
        res = res + jnp.where(sub == 0, down_y(gather(msgs, 1)), jnp.where(sub == 7, up_y(gather(msgs, 1)), 0.0))
        if s % 3 == 0:
            res = res + gather([RM[s, i] for i in range(3)], 2)
        if s % 3 == 2:
            res = res + gather([RM[s + 2, i] for i in range(3)], 2)
        return res

    start = []
    for s in range(15):
        v = CO[s, 0] * rhs(s)
        RO[s] = v
        start.append(v)
    e = dict(enumerate(start))
    for it in range(1, 6):
        new = {}
        for s in range(it, 15 - it):
            v = e[s]
            off = CO[s, 1] * e[s - 1] + CO[s, 2] * e[s + 1]
            off = off + CO[s, 3] * down_y(v) + CO[s, 4] * up_y(v)
            off = off + CO[s, 5] * pltpu.roll(v, 1, 1) + CO[s, 6] * pltpu.roll(v, 127, 1)
            new[s] = 0.2 * v + (RO[s] + off)
        e = new
    parts = []
    for s in range(5, 10):
        parts += [e[s], down_y(e[s]), up_y(e[s])]
    wide = dot(jnp.concatenate(parts, axis=0), px[...])

    for s in range(5):
        for h in range(2):
            mid, dn, up = (wide[24 * s + 8 * i : 24 * s + 8 * i + 8, 128 * h : 128 * h + 128] for i in range(3))
            lay = []
            for i in range(YV):
                v = mid
                if i < 4:
                    v = jnp.where(sub < 4 - i, dn, v)
                elif i > 4:
                    v = jnp.where(sub >= 12 - i, up, v)
                lay.append(v)
            lay = jnp.stack(lay, axis=0)
            lo, hi = ((0, 3), (3, 11), (11, 19), (19, 27), (27, 30))[s]

            def add(X, _, lay=lay, h=h):
                UA[X, h] = UB[X, h] + cs[X, h] * lay
                return 0

            lax.fori_loop(lo, hi, add, 0)

    def third(X):
        for h, v in enumerate(sweep(UA, X)):
            UB[X, h] = v

    def fourth(X):
        for h, v in enumerate(sweep(UB, X)):
            UA[X, h] = v

    def fifth(X):
        for h, v in enumerate(sweep(UA, X)):
            v = v * RC[X, h]
            for i in range(YV):
                on[X - XO, h, pl.ds(4 + i, 8, stride=9), :] = v[i]

    run(third, -2, 26)
    run(fourth, -1, 25)
    outs = []
    for n in range(4):
        run(fifth, 6 * n, 6 * n + 6)
        for h in range(2):
            cp = pltpu.make_async_copy(
                on.at[6 * n : 6 * n + 6, h, 8:72, :],
                out_ref.at[6 * n : 6 * n + 6, :, pl.ds(128 * h, 128)],
                out_sem.at[2 * n + h],
            )
            cp.start()
            outs.append(cp)
    for cp in outs:
        cp.wait()


def y_pair(ref, X, X2):
    return [y_total(ref[X, h] * ref[X2, h]) for h in range(2)]


def vmem(*shape):
    return pltpu.VMEM(shape, F32)


def shards(right_side, knudsen, solid):
    n_msg = 10 + 20 + 14 + 8
    scratch = [
        vmem(XL, 2, 64, 128), pltpu.VMEM((XL, 2, 64, 128), jnp.int32), vmem(30, 2, 80, 128), vmem(28, 2, 80, 128),
    ]
    scratch += [vmem(30, 2, YV, 8, 128) for _ in range(7)]
    scratch += [vmem(XL, 2, 80, 128)]
    scratch += [vmem(2, 240, 1, 128), vmem(2, 240, 1, 128), vmem(4, 10, 1, 128), vmem(4, 10, 1, 128)]
    scratch += [vmem(2, 144, 1, 128), vmem(2, 144, 1, 128), vmem(4, 8, 1, 128), vmem(4, 8, 1, 128)]
    scratch += [vmem(2, 3, 2, YV, 8, 128)]
    scratch += [
        vmem(3, 2, YV, 8, 128), vmem(3, 2, 8, 128), vmem(3, 2, YV, 8, 128), vmem(3, 2, YV, 8, 128),
        vmem(3, 2, YV, 8, 128), vmem(3, 2, 8, 128),
    ]
    scratch += [vmem(15, 3, 8, 128), vmem(17, 3, 8, 128), vmem(15, 7, 8, 128), vmem(15, 8, 128)]
    scratch += [vmem(256, 128), vmem(128, 256), vmem(256, 128)]
    scratch += [
        pltpu.SemaphoreType.DMA((6,)), pltpu.SemaphoreType.DMA((8,)),
        pltpu.SemaphoreType.DMA((n_msg,)), pltpu.SemaphoreType.DMA((n_msg,)),
    ]
    return pl.pallas_call(
        kernel,
        name="vcycle",
        out_shape=jax.ShapeDtypeStruct(right_side.shape, F32),
        in_specs=[pl.BlockSpec(memory_space=pl.ANY)] * 3,
        out_specs=pl.BlockSpec(memory_space=pl.ANY),
        scratch_shapes=scratch,
        compiler_params=pltpu.CompilerParams(
            collective_id=0, has_side_effects=True, vmem_limit_bytes=60 * 2**20
        ),
    )(knudsen, solid, right_side)


def solution(mesh):
    placed = P("region", "block", None)
    return jax.shard_map(shards, mesh=mesh, in_specs=(placed,) * 3, out_specs=placed, check_vma=False)
```

time: 385 us -> 55.5 us (0.14)
  the two profiles are of different devices: /device:TPU:135 before, /device:TPU:1 now
where the time goes in v1:
time: 55.5 us; the launch traced here: 55.4 us
  Pallas kernels  52.7 us (95%)
  local copies, waits for them, and re-layouts  2.7 us (5%)
    pallas_call x1, Pallas kernels, shards(): pl.pallas_call(kernel, name='vcycle', out_shape=jax.ShapeDtypeStruct(righ...  52.7 us
    unnamed x1, local copies, waits for them, and re-layouts  2.7 us

profile of v1, /device:TPU:1, one launch (start us, length us, event | category | flops | bytes accessed | tf_op | source)
XLA Modules:
  0.0 55.4 jit_solution(2705263267608444445)
XLA Ops:
  0.0 52.7 %vcycle.1 = f32[24,64,256]{2,1,0:T(8,128)} custom-call(f32[24,64,256]{2,1,0:T(8,128)} %k_ref.1, s32[24,64,256]{2,1,0:T(8,128)} %solid_ref.1, f32[24,64,256]{2,1,0:T(8,128)} %rs_ref.1), custom_call_target="tpu_custom_call" | custom-call | tf_op jit(solution)/shard_map/vcycle/pallas_call | solution.py:552
  52.7 2.7 %copy.5 = f32[24,64,256]{2,1,0:T(8,128)} copy(f32[24,64,256]{2,1,0:T(8,128)} %vcycle.1) | data formatting | bytes 3145728

commit v2 on v1

--- a/solution.py
+++ b/solution.py
@@ -135,7 +135,7 @@
             cn[x + XO, h, 8:72, :] = jnp.where(sn[x, h] == 0, k * lax.rsqrt(k), 0.0)
         return 0
 
-    lax.fori_loop(0, XL, root, 0)
+    lax.fori_loop(0, XL, root, 0, unroll=2)
     for cp in loads[4:]:
         cp.wait()
 
@@ -200,7 +200,7 @@
             cyacc[slab, h] += c[h] * y_sides(c[h])[0]
         return 0
 
-    lax.fori_loop(0, XL, deal, 0)
+    lax.fori_loop(0, XL, deal, 0, unroll=4)
 
     for cp in ymsg:
         cp.wait()
@@ -266,19 +266,24 @@
             racc[slab, h] += W[X, h] * (S[X, h] - RELAX * u[h] + G[X, h] * near[h])
             tacc[slab, h] += edge(cs[X, h]) * u[h][4]
 
-    def run(fn, lo, hi):
-        def body(X, _):
-            fn(X)
+    def run(fn, lo, hi, step=8):
+        whole = (hi - lo) // step
+
+        def body(i, _):
+            for j in range(step):
+                fn(lo + XO + i * step + j)
             return 0
 
-        lax.fori_loop(lo + XO, hi + XO, body, 0)
+        if whole:
+            lax.fori_loop(0, whole, body, 0)
+        for x in range(lo + whole * step, hi):
+            fn(x + XO)
 
     own_setup = functools.partial(setup, own=True)
-    halo_setup = functools.partial(setup, own=False)
-    run(own_setup, 1, 23)
-    run(first, 2, 22)
-    run(second, 3, 21)
-    run(resid, 4, 20)
+    run(own_setup, 1, 23, 8)
+    run(first, 2, 22, 7)
+    run(second, 3, 21, 6)
+    run(resid, 4, 20, 8)
 
     for cp in xmsg + cmsg:
         cp.wait()
@@ -299,16 +304,14 @@
         X, y = (1 if dr < 0 else 26), (7 if db < 0 else 72)
         for h in range(2):
             rn[X, h, y : y + 1, :] = crecv[n, 8 + h]
-    run(halo_setup, -2, 0)
-    run(own_setup, 0, 1)
-    run(own_setup, 23, 24)
-    run(halo_setup, 24, 26)
-    run(first, -1, 2)
-    run(first, 22, 25)
-    run(second, 0, 3)
-    run(second, 21, 24)
-    run(resid, 0, 4)
-    run(resid, 20, 24)
+    for x in (-2, -1, 0, 23, 24, 25):
+        setup(x + XO, 0 <= x < XL)
+    for x in (-1, 0, 1, 22, 23, 24):
+        first(x + XO)
+    for x in (0, 1, 2, 21, 22, 23):
+        second(x + XO)
+    for x in (0, 1, 2, 3, 20, 21, 22, 23):
+        resid(x + XO)
 
     def halves(fn):
         return jnp.concatenate([fn(0), fn(1)], axis=1)
@@ -374,39 +377,37 @@
     uxmsg = [remote(UB.at[3:6], xhalo.at[1], (-1, 0)), remote(UB.at[24:27], xhalo.at[0], (1, 0))]
     ucmsg = [remote(vsend.at[n], vrecv.at[3 - n], off) for n, off in enumerate(CORNERS)]
 
+    def turned(v, groups):
+        return pltpu.roll(v, groups % 4 * 32, v.ndim - 1) if groups % 4 else v
+
     def gather(msgs, g):
-        out = jnp.where(group == 2, pltpu.roll(msgs[2], (2 - g) % 4 * 32, 1) if g != 2 else msgs[2], 0.0)
-        out = jnp.where(group == 1, pltpu.roll(msgs[1], (1 - g) % 4 * 32, 1) if g != 1 else msgs[1], out)
-        return jnp.where(group == 0, pltpu.roll(msgs[0], (-g) % 4 * 32, 1) if g != 0 else msgs[0], out)
+        out = jnp.where(group == 2, turned(msgs[2], 2 - g), 0.0)
+        out = jnp.where(group == 1, turned(msgs[1], 1 - g), out)
+        return jnp.where(group == 0, turned(msgs[0], -g), out)
 
     def down_y(v):
-        t = pltpu.roll(v, 1, 0)
-        return jnp.where(sub == 0, pltpu.roll(t, 32, 1), t)
+        t = pltpu.roll(v, 1, v.ndim - 2)
+        return jnp.where(sub == 0, turned(t, 1), t)
 
     def up_y(v):
-        t = pltpu.roll(v, 7, 0)
-        return jnp.where(sub == 7, pltpu.roll(t, 96, 1), t)
+        t = pltpu.roll(v, 7, v.ndim - 2)
+        return jnp.where(sub == 7, turned(t, -1), t)
 
     for cp in kmsg:
         cp.wait()
 
-    def coarse(s, _):
-        msgs = [CM[s, i] for i in range(3)]
-        q = gather(msgs, 0)
-        cx = gather(msgs, 1)
-        cy = gather(msgs, 2)
-        cz = gather(msgs, 3)
-        after = gather([CM[jnp.minimum(s + 1, 14), i] for i in range(3)], 1)
-        CO[s, 0] = q
-        CO[s, 1] = q * cx
-        CO[s, 2] = q * after
-        CO[s, 3] = q * cy
-        CO[s, 4] = q * up_y(cy)
-        CO[s, 5] = q * cz
-        CO[s, 6] = q * jnp.where(group < 3, pltpu.roll(cz, 127, 1), 0.0)
-        return 0
-
-    lax.fori_loop(0, 15, coarse, 0)
+    msgs = [CM[:, i] for i in range(3)]
+    q = gather(msgs, 0)
+    cx = gather(msgs, 1)
+    cy = gather(msgs, 2)
+    cz = gather(msgs, 3)
+    CO[:, 0] = q
+    CO[:, 1] = q * cx
+    CO[0:14, 2] = q[0:14] * cx[1:15]
+    CO[:, 3] = q * cy
+    CO[:, 4] = q * up_y(cy)
+    CO[:, 5] = q * cz
+    CO[:, 6] = q * jnp.where(group < 3, pltpu.roll(cz, 127, 2), 0.0)
 
     for cp in uymsg + uxmsg + ucmsg:
         cp.wait()
@@ -440,19 +441,19 @@
     for cp in rmsg:
         cp.wait()
 
-    def rhs(s):
-        msgs = [RM[s + 1, i] for i in range(3)]
-        res = gather(msgs, 0)
-        res = res + jnp.where(sub == 0, down_y(gather(msgs, 1)), jnp.where(sub == 7, up_y(gather(msgs, 1)), 0.0))
-        if s % 3 == 0:
-            res = res + gather([RM[s, i] for i in range(3)], 2)
-        if s % 3 == 2:
-            res = res + gather([RM[s + 2, i] for i in range(3)], 2)
-        return res
-
+    msgs = [RM[:, i] for i in range(3)]
+    res = gather([m[1:16] for m in msgs], 0)
+    face = gather([m[1:16] for m in msgs], 1)
+    res = res + jnp.where(sub == 0, down_y(face), jnp.where(sub == 7, up_y(face), 0.0))
+    face = gather(msgs, 2)
     start = []
     for s in range(15):
-        v = CO[s, 0] * rhs(s)
+        v = res[s]
+        if s % 3 == 0:
+            v = v + face[s]
+        if s % 3 == 2:
+            v = v + face[s + 2]
+        v = CO[s, 0] * v
         RO[s] = v
         start.append(v)
     e = dict(enumerate(start))
@@ -504,11 +505,11 @@
             for i in range(YV):
                 on[X - XO, h, pl.ds(4 + i, 8, stride=9), :] = v[i]
 
-    run(third, -2, 26)
-    run(fourth, -1, 25)
+    run(third, -2, 26, 7)
+    run(fourth, -1, 25, 13)
     outs = []
     for n in range(4):
-        run(fifth, 6 * n, 6 * n + 6)
+        run(fifth, 6 * n, 6 * n + 6, 6)
         for h in range(2):
             cp = pltpu.make_async_copy(
                 on.at[6 * n : 6 * n + 6, h, 8:72, :],

time: 55.5 us -> 40.5 us (0.73)
  Pallas kernels: 52.7 us -> 37.7 us
    pallas_call x1, Pallas kernels: 52.7 us -> 37.7 us  [shards(): pl.pallas_call(kernel, name='vcycle', out_shape=jax.ShapeDtypeStruct(righ...]
where the time goes in v2:
time: 40.5 us; the launch traced here: 40.4 us
  Pallas kernels  37.7 us (93%)
  local copies, waits for them, and re-layouts  2.7 us (7%)
    pallas_call x1, Pallas kernels, shards(): pl.pallas_call(kernel, name='vcycle', out_shape=jax.ShapeDtypeStruct(righ...  37.7 us
    unnamed x1, local copies, waits for them, and re-layouts  2.7 us

profile of v2, /device:TPU:1, one launch (start us, length us, event | category | flops | bytes accessed | tf_op | source)
XLA Modules:
  0.0 40.4 jit_solution(11214235961191151494)
XLA Ops:
  0.0 37.7 %vcycle.1 = f32[24,64,256]{2,1,0:T(8,128)} custom-call(f32[24,64,256]{2,1,0:T(8,128)} %k_ref.1, s32[24,64,256]{2,1,0:T(8,128)} %solid_ref.1, f32[24,64,256]{2,1,0:T(8,128)} %rs_ref.1), custom_call_target="tpu_custom_call" | custom-call | tf_op jit(solution)/shard_map/vcycle/pallas_call | solution.py:553
  37.7 2.7 %copy.5 = f32[24,64,256]{2,1,0:T(8,128)} copy(f32[24,64,256]{2,1,0:T(8,128)} %vcycle.1) | data formatting | bytes 3145728

commit v3 on v2

--- a/solution.py
+++ b/solution.py
@@ -13,6 +13,8 @@
 XL = 24
 YV = 9
 XO = 3
+NCH, CH = 4, 6
+CROWS = CH * 6
 MASS = 0.05
 RELAX = 0.8
 
@@ -78,7 +80,7 @@
     kn, sn, cn, rn, cs, S, G, W, RC, UA, UB, on,
     ysend, yrecv, csend, crecv, usend, urecv, vsend, vrecv, xhalo,
     racc, tacc, cnt, czacc, cyacc, zacc, CM, RM, CO, RO, pz, px, po,
-    load_sem, out_sem, ss, rr,
+    rsn, EC, load_sem, out_sem, ss, rr,
 ):
     r = lax.axis_index("region")
     b = lax.axis_index("block")
@@ -91,11 +93,10 @@
         pl.semaphore_signal(bar, inc=1, device_id=dev(*off), device_id_type=MESH)
 
     loads = []
-    for i, (src, dst) in enumerate(((k_ref, kn), (solid_ref, sn), (rs_ref, rn.at[2 : 2 + XL, :, 8:72, :]))):
-        for h in range(2):
-            cp = pltpu.make_async_copy(
-                src.at[:, :, pl.ds(128 * h, 128)], dst.at[:, h], load_sem.at[2 * i + h]
-            )
+    for n in range(NCH):
+        part = pl.ds(n * CH, CH)
+        for i, (src, dst) in enumerate(((k_ref, kn), (solid_ref, sn), (rs_ref, rsn))):
+            cp = pltpu.make_async_copy(src.at[part], dst.at[part], load_sem.at[3 * n + i])
             cp.start()
             loads.append(cp)
 
@@ -126,44 +127,6 @@
             for ref in (tacc, zacc):
                 ref[s, h] = zero8
 
-    for cp in loads[:4]:
-        cp.wait()
-
-    def root(x, _):
-        for h in range(2):
-            k = kn[x, h]
-            cn[x + XO, h, 8:72, :] = jnp.where(sn[x, h] == 0, k * lax.rsqrt(k), 0.0)
-        return 0
-
-    lax.fori_loop(0, XL, root, 0, unroll=2)
-    for cp in loads[4:]:
-        cp.wait()
-
-    def pack(x, _):
-        for h in range(2):
-            for side in range(2):
-                for j in range(3):
-                    y = j if side == 0 else 61 + j
-                    ysend[side, (x * 2 + h) * 3 + j] = cn[x + XO, h, 8 + y : 9 + y, :]
-                for j in range(2):
-                    y = j if side == 0 else 62 + j
-                    ysend[side, 144 + (x * 2 + h) * 2 + j] = rn[x + 2, h, 8 + y : 9 + y, :]
-        return 0
-
-    lax.fori_loop(0, XL, pack, 0)
-    for n, (dr, db) in enumerate(CORNERS):
-        for p in range(2):
-            x = p if dr < 0 else XL - 2 + p
-            for h in range(2):
-                for j in range(2):
-                    y = j if db < 0 else 62 + j
-                    csend[n, (p * 2 + h) * 2 + j] = cn[x + XO, h, 8 + y : 9 + y, :]
-        x, y = 0 if dr < 0 else XL - 1, 0 if db < 0 else 63
-        for h in range(2):
-            csend[n, 8 + h] = rn[x + 2, h, 8 + y : 9 + y, :]
-
-    pl.semaphore_wait(bar, len(NEAR) + len(FAR))
-
     count = [0]
 
     def remote(src, dst, off):
@@ -176,7 +139,44 @@
         cp.start()
         return cp
 
-    ymsg = [remote(ysend.at[0], yrecv.at[1], (0, -1)), remote(ysend.at[1], yrecv.at[0], (0, 1))]
+    ymsg = []
+    for n in range(NCH):
+        for cp in loads[3 * n : 3 * n + 3]:
+            cp.wait()
+
+        def root(i, _, n=n):
+            x = n * CH + i
+            for h in range(2):
+                half = slice(128 * h, 128 * h + 128)
+                k = kn[x, :, half]
+                cn[x + XO, h, 8:72, :] = jnp.where(sn[x, :, half] == 0, k * lax.rsqrt(k), 0.0)
+                rn[x + 2, h, 8:72, :] = rsn[x, :, half]
+                for side in range(2):
+                    for j in range(3):
+                        y = j if side == 0 else 61 + j
+                        ysend[side, n, (i * 2 + h) * 3 + j] = cn[x + XO, h, 8 + y : 9 + y, :]
+                    for j in range(2):
+                        y = j if side == 0 else 62 + j
+                        ysend[side, n, CROWS + (i * 2 + h) * 2 + j] = rn[x + 2, h, 8 + y : 9 + y, :]
+            return 0
+
+        lax.fori_loop(0, CH, root, 0, unroll=2)
+        if n == 0:
+            pl.semaphore_wait(bar, len(NEAR) + len(FAR))
+        ymsg.append([
+            remote(ysend.at[0, n], yrecv.at[1, n], (0, -1)), remote(ysend.at[1, n], yrecv.at[0, n], (0, 1))
+        ])
+
+    for n, (dr, db) in enumerate(CORNERS):
+        for p in range(2):
+            x = p if dr < 0 else XL - 2 + p
+            for h in range(2):
+                for j in range(2):
+                    y = j if db < 0 else 62 + j
+                    csend[n, (p * 2 + h) * 2 + j] = cn[x + XO, h, 8 + y : 9 + y, :]
+        x, y = 0 if dr < 0 else XL - 1, 0 if db < 0 else 63
+        for h in range(2):
+            csend[n, 8 + h] = rn[x + 2, h, 8 + y : 9 + y, :]
     xmsg = [
         remote(cn.at[3:6, :, 8:72, :], cn.at[27:30, :, 8:72, :], (-1, 0)),
         remote(cn.at[24:27, :, 8:72, :], cn.at[0:3, :, 8:72, :], (1, 0)),
@@ -202,26 +202,48 @@
 
     lax.fori_loop(0, XL, deal, 0, unroll=4)
 
-    for cp in ymsg:
-        cp.wait()
+    vec, subs = iota(0, (YV, 8, 128)), iota(1, (YV, 8, 128))
+    place = subs * YV + vec
+    inside = (place >= 4) & (place < 68)
+    turn = lax.rem(vec + subs, 8) == 4
+
+    def halves(fn):
+        return jnp.concatenate([fn(0), fn(1)], axis=1)
+
+    def faces(X):
+        return halves(lambda h: y_total(cs[X, h] * cs[X + 1, h]))
+
+    parts = [halves(lambda h, s=s: y_total(cnt[s, h])) for s in range(3)]
+    parts += [halves(lambda h, s=s: y_total(jnp.where(turn, cyacc[s, h], 0.0))) for s in range(3)]
+    parts += [faces(10), faces(18)]
+    early = dot(jnp.concatenate(parts, axis=0), pz[...])
+    for i in range(8):
+        EC[i] = early[8 * i : 8 * i + 8]
+    early = dot(jnp.concatenate([halves(lambda h, s=s: y_total(czacc[s, h])) for s in range(3)], axis=0), po[...])
+    for i in range(3):
+        EC[8 + i] = early[8 * i : 8 * i + 8]
+
     below = jnp.where(b > 0, 1.0, 0.0).astype(F32)
     above = jnp.where(b < NBLK - 1, 1.0, 0.0).astype(F32)
     left = jnp.where(r > 0, 1.0, 0.0).astype(F32)
     right = jnp.where(r < NREG - 1, 1.0, 0.0).astype(F32)
 
-    def unpack(x, _):
-        for h in range(2):
-            at = (x * 2 + h) * 3
-            for j in range(3):
-                cs[x + XO, h, 1 + j, 0:1, :] = yrecv[0, at + j] * below
-                cs[x + XO, h, 5 + j, 7:8, :] = yrecv[1, at + j] * above
-            at = 144 + (x * 2 + h) * 2
-            for j in range(2):
-                rn[x + 2, h, 6 + j : 7 + j, :] = yrecv[0, at + j]
-                rn[x + 2, h, 72 + j : 73 + j, :] = yrecv[1, at + j]
-        return 0
-
-    lax.fori_loop(0, XL, unpack, 0)
+    def unpack(n):
+        def body(i, _):
+            x = n * CH + i
+            for h in range(2):
+                at = (i * 2 + h) * 3
+                for j in range(3):
+                    cs[x + XO, h, 1 + j, 0:1, :] = yrecv[0, n, at + j] * below
+                    cs[x + XO, h, 5 + j, 7:8, :] = yrecv[1, n, at + j] * above
+                at = CROWS + (i * 2 + h) * 2
+                for j in range(2):
+                    rn[x + 2, h, 6 + j : 7 + j, :] = yrecv[0, n, at + j]
+                    rn[x + 2, h, 72 + j : 73 + j, :] = yrecv[1, n, at + j]
+            return 0
+
+        lax.fori_loop(0, CH, body, 0, unroll=2)
+
     sub = iota(0)
 
     def edge(v):
@@ -251,10 +273,6 @@
         for h, v in enumerate(sweep(S, X)):
             UA[X, h] = v
 
-    vec, subs = iota(0, (YV, 8, 128)), iota(1, (YV, 8, 128))
-    place = subs * YV + vec
-    inside = (place >= 4) & (place < 68)
-
     def second(X):
         for h, v in enumerate(sweep(UA, X)):
             UB[X, h] = jnp.where(inside, v, 0.0)
@@ -280,7 +298,11 @@
             fn(x + XO)
 
     own_setup = functools.partial(setup, own=True)
-    run(own_setup, 1, 23, 8)
+    for n in range(NCH):
+        for cp in ymsg[n]:
+            cp.wait()
+        unpack(n)
+        run(own_setup, max(CH * n - 1, 1), CH * n + CH - 1, CH)
     run(first, 2, 22, 7)
     run(second, 3, 21, 6)
     run(resid, 4, 20, 8)
@@ -313,19 +335,18 @@
     for x in (0, 1, 2, 3, 20, 21, 22, 23):
         resid(x + XO)
 
-    def halves(fn):
-        return jnp.concatenate([fn(0), fn(1)], axis=1)
-
     parts = [halves(lambda h, s=s: y_total(racc[s, h])) for s in range(3)]
     parts += [halves(lambda h, s=s: tacc[s, h]) for s in range(3)]
     parts += [halves(lambda h: y_total(cs[2, h] * UB[3, h])), halves(lambda h: y_total(cs[27, h] * UB[26, h]))]
+    parts += [halves(lambda h, s=s: zacc[s, h]) for s in range(3)]
+    parts += [faces(2), faces(26)]
     tot = dot(jnp.concatenate(parts, axis=0), pz[...])
-    tot = [tot[8 * i : 8 * i + 8] for i in range(8)]
+    tot = [tot[8 * i : 8 * i + 8] for i in range(13)]
     group = lax.div(iota(1), 32)
-    faces = [tot[6], zero8, tot[7]]
+    ends = [tot[6], zero8, tot[7]]
     for s in range(3):
         RM[7 + s, 1] = jnp.where(
-            group == 0, tot[s], jnp.where(group == 1, tot[3 + s], jnp.where(group == 2, faces[s], 0.0))
+            group == 0, tot[s], jnp.where(group == 1, tot[3 + s], jnp.where(group == 2, ends[s], 0.0))
         )
     rmsg = [
         remote(RM.at[7:10, 1], RM.at[7 - 3 * dr : 10 - 3 * dr, 1 - db], (dr, db)) for dr, db in NEAR
@@ -334,23 +355,12 @@
         s, t = (9, 0) if dr > 0 else (7, 16)
         rmsg.append(remote(RM.at[s, 1], RM.at[t, 1 - db], (dr, db)))
 
-    planes = [y_pair(cs, 2, 3), y_pair(cs, 10, 11), y_pair(cs, 18, 19), y_pair(cs, 26, 27)]
-    parts = [halves(lambda h, s=s: y_total(cnt[s, h])) for s in range(3)]
-    parts += [halves(lambda h, p=p: p[h]) for p in planes]
-    turn = lax.rem(vec + subs, 8) == 4
-
-    def y_face(s, h):
-        return y_total(jnp.where(turn, cyacc[s, h], 0.0)) + jnp.where(sub == 0, zacc[s, h], 0.0)
-
-    parts += [halves(lambda h, s=s: y_face(s, h)) for s in range(3)]
-    parts += [halves(lambda h, s=s: zacc[s, h]) for s in range(3)]
-    tot = dot(jnp.concatenate(parts, axis=0), pz[...])
-    tot = [tot[8 * i : 8 * i + 8] for i in range(13)]
-    tz = dot(jnp.concatenate([halves(lambda h, s=s: y_total(czacc[s, h])) for s in range(3)], axis=0), po[...])
+    cxs = [tot[11], EC[6], EC[7], tot[12]]
     for s in range(3):
-        cx, cx2, cy, cz = tot[3 + s], tot[4 + s], tot[7 + s], tz[8 * s : 8 * s + 8]
-        cy2 = jnp.where(sub == 7, tot[10 + s], pltpu.roll(cy, 7, 0))
-        diag = MASS * (tot[s] + 1.0) + cx + cx2 + cy + cy2 + cz + pltpu.roll(cz, 127, 1)
+        face = tot[8 + s]
+        cx, cx2, cy, cz = cxs[s], cxs[s + 1], EC[3 + s] + jnp.where(sub == 0, face, 0.0), EC[8 + s]
+        cy2 = jnp.where(sub == 7, face, pltpu.roll(cy, 7, 0))
+        diag = MASS * (EC[s] + 1.0) + cx + cx2 + cy + cy2 + cz + pltpu.roll(cz, 127, 1)
         CM[6 + s, 1] = jnp.where(
             group == 0, RELAX / diag, jnp.where(group == 1, cx, jnp.where(group == 2, cy, cz))
         )
@@ -522,22 +532,18 @@
         cp.wait()
 
 
-def y_pair(ref, X, X2):
-    return [y_total(ref[X, h] * ref[X2, h]) for h in range(2)]
-
-
 def vmem(*shape):
     return pltpu.VMEM(shape, F32)
 
 
 def shards(right_side, knudsen, solid):
-    n_msg = 10 + 20 + 14 + 8
+    n_msg = 2 * NCH + 8 + 20 + 14 + 8
     scratch = [
-        vmem(XL, 2, 64, 128), pltpu.VMEM((XL, 2, 64, 128), jnp.int32), vmem(30, 2, 80, 128), vmem(28, 2, 80, 128),
+        vmem(XL, 64, 256), pltpu.VMEM((XL, 64, 256), jnp.int32), vmem(30, 2, 80, 128), vmem(28, 2, 80, 128),
     ]
     scratch += [vmem(30, 2, YV, 8, 128) for _ in range(7)]
     scratch += [vmem(XL, 2, 80, 128)]
-    scratch += [vmem(2, 240, 1, 128), vmem(2, 240, 1, 128), vmem(4, 10, 1, 128), vmem(4, 10, 1, 128)]
+    scratch += [vmem(2, NCH, CH * 10, 1, 128), vmem(2, NCH, CH * 10, 1, 128), vmem(4, 10, 1, 128), vmem(4, 10, 1, 128)]
     scratch += [vmem(2, 144, 1, 128), vmem(2, 144, 1, 128), vmem(4, 8, 1, 128), vmem(4, 8, 1, 128)]
     scratch += [vmem(2, 3, 2, YV, 8, 128)]
     scratch += [
@@ -545,20 +551,20 @@
         vmem(3, 2, YV, 8, 128), vmem(3, 2, 8, 128),
     ]
     scratch += [vmem(15, 3, 8, 128), vmem(17, 3, 8, 128), vmem(15, 7, 8, 128), vmem(15, 8, 128)]
-    scratch += [vmem(256, 128), vmem(128, 256), vmem(256, 128)]
+    scratch += [vmem(256, 128), vmem(128, 256), vmem(256, 128), vmem(XL, 64, 256), vmem(11, 8, 128)]
     scratch += [
-        pltpu.SemaphoreType.DMA((6,)), pltpu.SemaphoreType.DMA((8,)),
+        pltpu.SemaphoreType.DMA((3 * NCH,)), pltpu.SemaphoreType.DMA((8,)),
         pltpu.SemaphoreType.DMA((n_msg,)), pltpu.SemaphoreType.DMA((n_msg,)),
     ]
     return pl.pallas_call(
         kernel,
         name="vcycle",
-        out_shape=jax.ShapeDtypeStruct(right_side.shape, F32),
-        in_specs=[pl.BlockSpec(memory_space=pl.ANY)] * 3,
-        out_specs=pl.BlockSpec(memory_space=pl.ANY),
+        out_shape=pltpu.VMEM(right_side.shape, F32),
+        in_specs=[pl.BlockSpec(memory_space=pltpu.HBM)] * 3,
+        out_specs=pl.BlockSpec(memory_space=pltpu.VMEM),
         scratch_shapes=scratch,
         compiler_params=pltpu.CompilerParams(
-            collective_id=0, has_side_effects=True, vmem_limit_bytes=60 * 2**20
+            collective_id=0, has_side_effects=True, vmem_limit_bytes=58 * 2**20
         ),
     )(knudsen, solid, right_side)
 

time: 40.5 us -> 37.3 us (0.921)
  Pallas kernels: 37.7 us -> 36 us
  local copies, waits for them, and re-layouts: 2.7 us -> 1.15 us
    pallas_call x1, Pallas kernels: 37.7 us -> 36 us  [shards(): pl.pallas_call(kernel, name='vcycle', out_shape=pltpu.VMEM(right_side.sha...]
    unnamed x1, local copies, waits for them, and re-layouts: 2.7 us -> 1.15 us
where the time goes in v3:
time: 37.3 us; the launch traced here: 37.2 us
  Pallas kernels  36 us (97%)
  local copies, waits for them, and re-layouts  1.15 us (3%)
    pallas_call x1, Pallas kernels, shards(): pl.pallas_call(kernel, name='vcycle', out_shape=pltpu.VMEM(right_side.sha...  36 us
    unnamed x1, local copies, waits for them, and re-layouts  1.15 us

profile of v3, /device:TPU:1, one launch (start us, length us, event | category | flops | bytes accessed | tf_op | source)
XLA Modules:
  0.0 37.2 jit_solution(15669521550098579748)
XLA Ops:
  0.0 36.0 %vcycle.1 = f32[24,64,256]{2,1,0:T(8,128)S(1)} custom-call(f32[24,64,256]{2,1,0:T(8,128)} %k_ref.1, s32[24,64,256]{2,1,0:T(8,128)} %solid_ref.1, f32[24,64,256]{2,1,0:T(8,128)} %rs_ref.1), custom_call_target="tpu_custom_call" | custom-call | tf_op jit(solution)/shard_map/vcycle/pallas_call | solution.py:559
  36.0 1.1 %copy.5 = f32[24,64,256]{2,1,0:T(8,128)} copy(f32[24,64,256]{2,1,0:T(8,128)S(1)} %vcycle.1) | data formatting | bytes 3145728

commit v4 on v3

--- a/solution.py
+++ b/solution.py
@@ -80,7 +80,7 @@
     kn, sn, cn, rn, cs, S, G, W, RC, UA, UB, on,
     ysend, yrecv, csend, crecv, usend, urecv, vsend, vrecv, xhalo,
     racc, tacc, cnt, czacc, cyacc, zacc, CM, RM, CO, RO, pz, px, po,
-    rsn, EC, load_sem, out_sem, ss, rr,
+    rsn, EC, wide, LAY, UC, load_sem, out_sem, ss, rr,
 ):
     r = lax.axis_index("region")
     b = lax.axis_index("block")
@@ -213,20 +213,28 @@
     def faces(X):
         return halves(lambda h: y_total(cs[X, h] * cs[X + 1, h]))
 
-    parts = [halves(lambda h, s=s: y_total(cnt[s, h])) for s in range(3)]
-    parts += [halves(lambda h, s=s: y_total(jnp.where(turn, cyacc[s, h], 0.0))) for s in range(3)]
-    parts += [faces(10), faces(18)]
-    early = dot(jnp.concatenate(parts, axis=0), pz[...])
-    for i in range(8):
-        EC[i] = early[8 * i : 8 * i + 8]
-    early = dot(jnp.concatenate([halves(lambda h, s=s: y_total(czacc[s, h])) for s in range(3)], axis=0), po[...])
-    for i in range(3):
-        EC[8 + i] = early[8 * i : 8 * i + 8]
+    def early_sums():
+        parts = [halves(lambda h, s=s: y_total(cnt[s, h])) for s in range(3)]
+        parts += [halves(lambda h, s=s: y_total(jnp.where(turn, cyacc[s, h], 0.0))) for s in range(3)]
+        parts += [faces(10), faces(18)]
+        early = dot(jnp.concatenate(parts, axis=0), pz[...])
+        for i in range(8):
+            EC[i] = early[8 * i : 8 * i + 8]
+        early = dot(jnp.concatenate([halves(lambda h, s=s: y_total(czacc[s, h])) for s in range(3)], axis=0), po[...])
+        for i in range(3):
+            EC[8 + i] = early[8 * i : 8 * i + 8]
+
+    early_sums()
 
     below = jnp.where(b > 0, 1.0, 0.0).astype(F32)
     above = jnp.where(b < NBLK - 1, 1.0, 0.0).astype(F32)
     left = jnp.where(r > 0, 1.0, 0.0).astype(F32)
     right = jnp.where(r < NREG - 1, 1.0, 0.0).astype(F32)
+
+    sub = iota(0)
+
+    def edge(v):
+        return jnp.where(sub == 0, v[3], jnp.where(sub == 7, v[5], 0.0))
 
     def unpack(n):
         def body(i, _):
@@ -240,14 +248,10 @@
                 for j in range(2):
                     rn[x + 2, h, 6 + j : 7 + j, :] = yrecv[0, n, at + j]
                     rn[x + 2, h, 72 + j : 73 + j, :] = yrecv[1, n, at + j]
+                zacc[lax.div(x, 8), h] += edge(cs[x + XO, h]) * cs[x + XO, h, 4]
             return 0
 
         lax.fori_loop(0, CH, body, 0, unroll=2)
-
-    sub = iota(0)
-
-    def edge(v):
-        return jnp.where(sub == 0, v[3], jnp.where(sub == 7, v[5], 0.0))
 
     def setup(X, own):
         c, near = around(cs, X)
@@ -263,7 +267,6 @@
                 rc = jnp.where(pore, both * d, 0.0)
                 RC[X, h] = rc
                 W[X, h] = (1.0 / RELAX) * d * rc
-                zacc[lax.div(X - XO, 8), h] += edge(c[h]) * c[h][4]
 
     def sweep(src, X):
         u, near = around(src, X)
@@ -309,64 +312,78 @@
 
     for cp in xmsg + cmsg:
         cp.wait()
-    for X, side in ((0, left), (1, left), (2, left), (27, right), (28, right), (29, right)):
-        for h in range(2):
-            cs[X, h] = strided(cn, X, h) * side
-    for n, (dr, db) in enumerate(CORNERS):
-        side = (left if dr < 0 else right) * (below if db < 0 else above)
-        for p in range(2):
-            X = (1 + p) if dr < 0 else (27 + p)
+    def x_halo():
+        for X, side in ((0, left), (1, left), (2, left), (27, right), (28, right), (29, right)):
             for h in range(2):
-                for j in range(2):
-                    v = crecv[n, (p * 2 + h) * 2 + j] * side
-                    if db < 0:
-                        cs[X, h, 2 + j, 0:1, :] = v
-                    else:
-                        cs[X, h, 5 + j, 7:8, :] = v
-        X, y = (1 if dr < 0 else 26), (7 if db < 0 else 72)
-        for h in range(2):
-            rn[X, h, y : y + 1, :] = crecv[n, 8 + h]
-    for x in (-2, -1, 0, 23, 24, 25):
-        setup(x + XO, 0 <= x < XL)
-    for x in (-1, 0, 1, 22, 23, 24):
-        first(x + XO)
-    for x in (0, 1, 2, 21, 22, 23):
-        second(x + XO)
-    for x in (0, 1, 2, 3, 20, 21, 22, 23):
-        resid(x + XO)
-
-    parts = [halves(lambda h, s=s: y_total(racc[s, h])) for s in range(3)]
-    parts += [halves(lambda h, s=s: tacc[s, h]) for s in range(3)]
-    parts += [halves(lambda h: y_total(cs[2, h] * UB[3, h])), halves(lambda h: y_total(cs[27, h] * UB[26, h]))]
-    parts += [halves(lambda h, s=s: zacc[s, h]) for s in range(3)]
-    parts += [faces(2), faces(26)]
-    tot = dot(jnp.concatenate(parts, axis=0), pz[...])
-    tot = [tot[8 * i : 8 * i + 8] for i in range(13)]
+                cs[X, h] = strided(cn, X, h) * side
+        for n, (dr, db) in enumerate(CORNERS):
+            side = (left if dr < 0 else right) * (below if db < 0 else above)
+            for p in range(2):
+                X = (1 + p) if dr < 0 else (27 + p)
+                for h in range(2):
+                    for j in range(2):
+                        v = crecv[n, (p * 2 + h) * 2 + j] * side
+                        if db < 0:
+                            cs[X, h, 2 + j, 0:1, :] = v
+                        else:
+                            cs[X, h, 5 + j, 7:8, :] = v
+            X, y = (1 if dr < 0 else 26), (7 if db < 0 else 72)
+            for h in range(2):
+                rn[X, h, y : y + 1, :] = crecv[n, 8 + h]
+
+    x_halo()
     group = lax.div(iota(1), 32)
-    ends = [tot[6], zero8, tot[7]]
-    for s in range(3):
-        RM[7 + s, 1] = jnp.where(
-            group == 0, tot[s], jnp.where(group == 1, tot[3 + s], jnp.where(group == 2, ends[s], 0.0))
-        )
+
+    def conductances():
+        parts = [halves(lambda h, s=s: zacc[s, h]) for s in range(3)] + [faces(2), faces(26)]
+        tot = dot(jnp.concatenate(parts, axis=0), pz[...])
+        tot = [tot[8 * i : 8 * i + 8] for i in range(5)]
+        cxs = [tot[3], EC[6], EC[7], tot[4]]
+        for s in range(3):
+            face = tot[s]
+            cx, cx2, cy, cz = cxs[s], cxs[s + 1], EC[3 + s] + jnp.where(sub == 0, face, 0.0), EC[8 + s]
+            cy2 = jnp.where(sub == 7, face, pltpu.roll(cy, 7, 0))
+            diag = MASS * (EC[s] + 1.0) + cx + cx2 + cy + cy2 + cz + pltpu.roll(cz, 127, 1)
+            CM[6 + s, 1] = jnp.where(
+                group == 0, RELAX / diag, jnp.where(group == 1, cx, jnp.where(group == 2, cy, cz))
+            )
+
+    conductances()
+    kmsg = [
+        remote(CM.at[6:9, 1], CM.at[6 - 3 * dr : 9 - 3 * dr, 1 - db], (dr, db)) for dr, db in NEAR
+    ]
+
+    def ends():
+        for x in (-2, -1, 0, 23, 24, 25):
+            setup(x + XO, 0 <= x < XL)
+        for x in (-1, 0, 1, 22, 23, 24):
+            first(x + XO)
+        for x in (0, 1, 2, 21, 22, 23):
+            second(x + XO)
+        for x in (0, 1, 2, 3, 20, 21, 22, 23):
+            resid(x + XO)
+
+    ends()
+
+    def residual_sums():
+        parts = [halves(lambda h, s=s: y_total(racc[s, h])) for s in range(3)]
+        parts += [halves(lambda h, s=s: tacc[s, h]) for s in range(3)]
+        parts += [halves(lambda h: y_total(cs[2, h] * UB[3, h])), halves(lambda h: y_total(cs[27, h] * UB[26, h]))]
+        tot = dot(jnp.concatenate(parts, axis=0), pz[...])
+        tot = [tot[8 * i : 8 * i + 8] for i in range(8)]
+        end = [tot[6], zero8, tot[7]]
+        for s in range(3):
+            RM[7 + s, 1] = jnp.where(
+                group == 0, tot[s], jnp.where(group == 1, tot[3 + s], jnp.where(group == 2, end[s], 0.0))
+            )
+
+    residual_sums()
     rmsg = [
         remote(RM.at[7:10, 1], RM.at[7 - 3 * dr : 10 - 3 * dr, 1 - db], (dr, db)) for dr, db in NEAR
     ]
     for dr, db in FAR:
         s, t = (9, 0) if dr > 0 else (7, 16)
         rmsg.append(remote(RM.at[s, 1], RM.at[t, 1 - db], (dr, db)))
-
-    cxs = [tot[11], EC[6], EC[7], tot[12]]
-    for s in range(3):
-        face = tot[8 + s]
-        cx, cx2, cy, cz = cxs[s], cxs[s + 1], EC[3 + s] + jnp.where(sub == 0, face, 0.0), EC[8 + s]
-        cy2 = jnp.where(sub == 7, face, pltpu.roll(cy, 7, 0))
-        diag = MASS * (EC[s] + 1.0) + cx + cx2 + cy + cy2 + cz + pltpu.roll(cz, 127, 1)
-        CM[6 + s, 1] = jnp.where(
-            group == 0, RELAX / diag, jnp.where(group == 1, cx, jnp.where(group == 2, cy, cz))
-        )
-    kmsg = [
-        remote(CM.at[6:9, 1], CM.at[6 - 3 * dr : 9 - 3 * dr, 1 - db], (dr, db)) for dr, db in NEAR
-    ]
 
     def upack(x, _):
         for h in range(2):
@@ -406,18 +423,21 @@
     for cp in kmsg:
         cp.wait()
 
-    msgs = [CM[:, i] for i in range(3)]
-    q = gather(msgs, 0)
-    cx = gather(msgs, 1)
-    cy = gather(msgs, 2)
-    cz = gather(msgs, 3)
-    CO[:, 0] = q
-    CO[:, 1] = q * cx
-    CO[0:14, 2] = q[0:14] * cx[1:15]
-    CO[:, 3] = q * cy
-    CO[:, 4] = q * up_y(cy)
-    CO[:, 5] = q * cz
-    CO[:, 6] = q * jnp.where(group < 3, pltpu.roll(cz, 127, 2), 0.0)
+    def coefficients():
+        msgs = [CM[:, i] for i in range(3)]
+        q = gather(msgs, 0)
+        cx = gather(msgs, 1)
+        cy = gather(msgs, 2)
+        cz = gather(msgs, 3)
+        CO[:, 0] = q
+        CO[:, 1] = q * cx
+        CO[0:14, 2] = q[0:14] * cx[1:15]
+        CO[:, 3] = q * cy
+        CO[:, 4] = q * up_y(cy)
+        CO[:, 5] = q * cz
+        CO[:, 6] = q * jnp.where(group < 3, pltpu.roll(cz, 127, 2), 0.0)
+
+    coefficients()
 
     for cp in uymsg + uxmsg + ucmsg:
         cp.wait()
@@ -430,56 +450,62 @@
         return 0
 
     lax.fori_loop(0, XL, uunpack, 0)
-    for X, n, i, side in (
-        (0, 0, 0, left), (1, 0, 1, left), (2, 0, 2, left),
-        (27, 1, 0, right), (28, 1, 1, right), (29, 1, 2, right),
-    ):
-        for h in range(2):
-            UB[X, h] = xhalo[n, i, h] * side
-    for n, (dr, db) in enumerate(CORNERS):
-        side = (left if dr < 0 else right) * (below if db < 0 else above)
-        for p in range(2):
-            X = (1 + p) if dr < 0 else (27 + p)
+    def u_halo():
+        for X, n, i, side in (
+            (0, 0, 0, left), (1, 0, 1, left), (2, 0, 2, left),
+            (27, 1, 0, right), (28, 1, 1, right), (29, 1, 2, right),
+        ):
             for h in range(2):
-                for j in range(2):
-                    v = vrecv[n, (p * 2 + h) * 2 + j] * side
-                    if db < 0:
-                        UB[X, h, 2 + j, 0:1, :] = v
-                    else:
-                        UB[X, h, 5 + j, 7:8, :] = v
+                UB[X, h] = xhalo[n, i, h] * side
+        for n, (dr, db) in enumerate(CORNERS):
+            side = (left if dr < 0 else right) * (below if db < 0 else above)
+            for p in range(2):
+                X = (1 + p) if dr < 0 else (27 + p)
+                for h in range(2):
+                    for j in range(2):
+                        v = vrecv[n, (p * 2 + h) * 2 + j] * side
+                        if db < 0:
+                            UB[X, h, 2 + j, 0:1, :] = v
+                        else:
+                            UB[X, h, 5 + j, 7:8, :] = v
+
+    u_halo()
 
     for cp in rmsg:
         cp.wait()
 
-    msgs = [RM[:, i] for i in range(3)]
-    res = gather([m[1:16] for m in msgs], 0)
-    face = gather([m[1:16] for m in msgs], 1)
-    res = res + jnp.where(sub == 0, down_y(face), jnp.where(sub == 7, up_y(face), 0.0))
-    face = gather(msgs, 2)
-    start = []
-    for s in range(15):
-        v = res[s]
-        if s % 3 == 0:
-            v = v + face[s]
-        if s % 3 == 2:
-            v = v + face[s + 2]
-        v = CO[s, 0] * v
-        RO[s] = v
-        start.append(v)
-    e = dict(enumerate(start))
-    for it in range(1, 6):
-        new = {}
-        for s in range(it, 15 - it):
-            v = e[s]
-            off = CO[s, 1] * e[s - 1] + CO[s, 2] * e[s + 1]
-            off = off + CO[s, 3] * down_y(v) + CO[s, 4] * up_y(v)
-            off = off + CO[s, 5] * pltpu.roll(v, 1, 1) + CO[s, 6] * pltpu.roll(v, 127, 1)
-            new[s] = 0.2 * v + (RO[s] + off)
-        e = new
-    parts = []
-    for s in range(5, 10):
-        parts += [e[s], down_y(e[s]), up_y(e[s])]
-    wide = dot(jnp.concatenate(parts, axis=0), px[...])
+    def solve():
+        msgs = [RM[:, i] for i in range(3)]
+        res = gather([m[1:16] for m in msgs], 0)
+        face = gather([m[1:16] for m in msgs], 1)
+        res = res + jnp.where(sub == 0, down_y(face), jnp.where(sub == 7, up_y(face), 0.0))
+        face = gather(msgs, 2)
+        start = []
+        for s in range(15):
+            v = res[s]
+            if s % 3 == 0:
+                v = v + face[s]
+            if s % 3 == 2:
+                v = v + face[s + 2]
+            v = CO[s, 0] * v
+            RO[s] = v
+            start.append(v)
+        e = dict(enumerate(start))
+        for it in range(1, 6):
+            new = {}
+            for s in range(it, 15 - it):
+                v = e[s]
+                off = CO[s, 1] * e[s - 1] + CO[s, 2] * e[s + 1]
+                off = off + CO[s, 3] * down_y(v) + CO[s, 4] * up_y(v)
+                off = off + CO[s, 5] * pltpu.roll(v, 1, 1) + CO[s, 6] * pltpu.roll(v, 127, 1)
+                new[s] = 0.2 * v + (RO[s] + off)
+            e = new
+        parts = []
+        for s in range(5, 10):
+            parts += [e[s], down_y(e[s]), up_y(e[s])]
+        wide[...] = dot(jnp.concatenate(parts, axis=0), px[...])
+
+    solve()
 
     for s in range(5):
         for h in range(2):
@@ -493,20 +519,19 @@
                     v = jnp.where(sub >= 12 - i, up, v)
                 lay.append(v)
             lay = jnp.stack(lay, axis=0)
-            lo, hi = ((0, 3), (3, 11), (11, 19), (19, 27), (27, 30))[s]
-
-            def add(X, _, lay=lay, h=h):
-                UA[X, h] = UB[X, h] + cs[X, h] * lay
-                return 0
-
-            lax.fori_loop(lo, hi, add, 0)
+            LAY[s, h] = lay
+
+    def add(X):
+        for h in range(2):
+            UA[X, h] = UB[X, h] + cs[X, h] * LAY[lax.div(X + 5, 8), h]
 
     def third(X):
+        add(X + 1)
         for h, v in enumerate(sweep(UA, X)):
-            UB[X, h] = v
+            UC[X, h] = v
 
     def fourth(X):
-        for h, v in enumerate(sweep(UB, X)):
+        for h, v in enumerate(sweep(UC, X)):
             UA[X, h] = v
 
     def fifth(X):
@@ -515,6 +540,8 @@
             for i in range(YV):
                 on[X - XO, h, pl.ds(4 + i, 8, stride=9), :] = v[i]
 
+    add(0)
+    add(1)
     run(third, -2, 26, 7)
     run(fourth, -1, 25, 13)
     outs = []
@@ -551,7 +578,7 @@
         vmem(3, 2, YV, 8, 128), vmem(3, 2, 8, 128),
     ]
     scratch += [vmem(15, 3, 8, 128), vmem(17, 3, 8, 128), vmem(15, 7, 8, 128), vmem(15, 8, 128)]
-    scratch += [vmem(256, 128), vmem(128, 256), vmem(256, 128), vmem(XL, 64, 256), vmem(11, 8, 128)]
+    scratch += [vmem(256, 128), vmem(128, 256), vmem(256, 128), vmem(XL, 64, 256), vmem(11, 8, 128), vmem(120, 256), vmem(5, 2, YV, 8, 128), vmem(30, 2, YV, 8, 128)]
     scratch += [
         pltpu.SemaphoreType.DMA((3 * NCH,)), pltpu.SemaphoreType.DMA((8,)),
         pltpu.SemaphoreType.DMA((n_msg,)), pltpu.SemaphoreType.DMA((n_msg,)),

time: 37.3 us -> 36.5 us (0.979)
  Pallas kernels: 36 us -> 35.3 us
    pallas_call x1, Pallas kernels: 36 us -> 35.3 us  [shards(): pl.pallas_call(kernel, name='vcycle', out_shape=pltpu.VMEM(right_side.sha...]
where the time goes in v4:
time: 36.5 us
  Pallas kernels  35.3 us (97%)
  local copies, waits for them, and re-layouts  1.15 us (3%)
    pallas_call x1, Pallas kernels, shards(): pl.pallas_call(kernel, name='vcycle', out_shape=pltpu.VMEM(right_side.sha...  35.3 us
    unnamed x1, local copies, waits for them, and re-layouts  1.15 us

profile of v4, /device:TPU:1, one launch (start us, length us, event | category | flops | bytes accessed | tf_op | source)
XLA Modules:
  0.0 36.5 jit_solution(475776144928284963)
XLA Ops:
  0.0 35.3 %vcycle.1 = f32[24,64,256]{2,1,0:T(8,128)S(1)} custom-call(f32[24,64,256]{2,1,0:T(8,128)} %k_ref.1, s32[24,64,256]{2,1,0:T(8,128)} %solid_ref.1, f32[24,64,256]{2,1,0:T(8,128)} %rs_ref.1), custom_call_target="tpu_custom_call" | custom-call | tf_op jit(solution)/shard_map/vcycle/pallas_call | solution.py:586
  35.3 1.1 %copy.5 = f32[24,64,256]{2,1,0:T(8,128)} copy(f32[24,64,256]{2,1,0:T(8,128)S(1)} %vcycle.1) | data formatting | bytes 3145728

commit v5 on v4

--- a/solution.py
+++ b/solution.py
@@ -80,7 +80,7 @@
     kn, sn, cn, rn, cs, S, G, W, RC, UA, UB, on,
     ysend, yrecv, csend, crecv, usend, urecv, vsend, vrecv, xhalo,
     racc, tacc, cnt, czacc, cyacc, zacc, CM, RM, CO, RO, pz, px, po,
-    rsn, EC, wide, LAY, UC, load_sem, out_sem, ss, rr,
+    rsn, EC, wide, LAY, UC, load_sem, ss, rr,
 ):
     r = lax.axis_index("region")
     b = lax.axis_index("block")
@@ -439,7 +439,9 @@
 
     coefficients()
 
-    for cp in uymsg + uxmsg + ucmsg:
+    for cp in uxmsg:
+        cp.wait_send()
+    for cp in uymsg:
         cp.wait()
 
     def uunpack(x, _):
@@ -468,8 +470,6 @@
                             UB[X, h, 2 + j, 0:1, :] = v
                         else:
                             UB[X, h, 5 + j, 7:8, :] = v
-
-    u_halo()
 
     for cp in rmsg:
         cp.wait()
@@ -507,6 +507,12 @@
 
     solve()
 
+    for cp in uxmsg:
+        cp.wait_recv()
+    for cp in ucmsg:
+        cp.wait()
+    u_halo()
+
     for s in range(5):
         for h in range(2):
             mid, dn, up = (wide[24 * s + 8 * i : 24 * s + 8 * i + 8, 128 * h : 128 * h + 128] for i in range(3))
@@ -539,24 +545,13 @@
             v = v * RC[X, h]
             for i in range(YV):
                 on[X - XO, h, pl.ds(4 + i, 8, stride=9), :] = v[i]
+            out_ref[X - XO, :, 128 * h : 128 * h + 128] = on[X - XO, h, 8:72, :]
 
     add(0)
     add(1)
     run(third, -2, 26, 7)
     run(fourth, -1, 25, 13)
-    outs = []
-    for n in range(4):
-        run(fifth, 6 * n, 6 * n + 6, 6)
-        for h in range(2):
-            cp = pltpu.make_async_copy(
-                on.at[6 * n : 6 * n + 6, h, 8:72, :],
-                out_ref.at[6 * n : 6 * n + 6, :, pl.ds(128 * h, 128)],
-                out_sem.at[2 * n + h],
-            )
-            cp.start()
-            outs.append(cp)
-    for cp in outs:
-        cp.wait()
+    run(fifth, 0, XL, 8)
 
 
 def vmem(*shape):
@@ -580,7 +575,7 @@
     scratch += [vmem(15, 3, 8, 128), vmem(17, 3, 8, 128), vmem(15, 7, 8, 128), vmem(15, 8, 128)]
     scratch += [vmem(256, 128), vmem(128, 256), vmem(256, 128), vmem(XL, 64, 256), vmem(11, 8, 128), vmem(120, 256), vmem(5, 2, YV, 8, 128), vmem(30, 2, YV, 8, 128)]
     scratch += [
-        pltpu.SemaphoreType.DMA((3 * NCH,)), pltpu.SemaphoreType.DMA((8,)),
+        pltpu.SemaphoreType.DMA((3 * NCH,)),
         pltpu.SemaphoreType.DMA((n_msg,)), pltpu.SemaphoreType.DMA((n_msg,)),
     ]
     return pl.pallas_call(

time: 36.5 us -> 35.4 us (0.970)
  Pallas kernels: 35.3 us -> 34.2 us
    pallas_call x1, Pallas kernels: 35.3 us -> 34.2 us  [shards(): pl.pallas_call(kernel, name='vcycle', out_shape=pltpu.VMEM(right_side.sha...]
where the time goes in v5:
time: 35.4 us; the launch traced here: 35.3 us
  Pallas kernels  34.2 us (97%)
  local copies, waits for them, and re-layouts  1.15 us (3%)
    pallas_call x1, Pallas kernels, shards(): pl.pallas_call(kernel, name='vcycle', out_shape=pltpu.VMEM(right_side.sha...  34.2 us
    unnamed x1, local copies, waits for them, and re-layouts  1.15 us

profile of v5, /device:TPU:1, one launch (start us, length us, event | category | flops | bytes accessed | tf_op | source)
XLA Modules:
  0.0 35.3 jit_solution(27093383314471891)
XLA Ops:
  0.0 34.2 %vcycle.1 = f32[24,64,256]{2,1,0:T(8,128)S(1)} custom-call(f32[24,64,256]{2,1,0:T(8,128)} %k_ref.1, s32[24,64,256]{2,1,0:T(8,128)} %solid_ref.1, f32[24,64,256]{2,1,0:T(8,128)} %rs_ref.1), custom_call_target="tpu_custom_call" | custom-call | tf_op jit(solution)/shard_map/vcycle/pallas_call | solution.py:581
  34.2 1.1 %copy.5 = f32[24,64,256]{2,1,0:T(8,128)} copy(f32[24,64,256]{2,1,0:T(8,128)S(1)} %vcycle.1) | data formatting | bytes 3145728

commit v6 on v5

--- a/solution.py
+++ b/solution.py
@@ -18,7 +18,7 @@
 MASS = 0.05
 RELAX = 0.8
 
-NEAR = [(dr, db) for dr in (-2, -1, 0, 1, 2) for db in (-1, 0, 1) if (dr, db) != (0, 0)]
+NEAR = [(dr, db) for dr in (-2, 2, -1, 1, 0) for db in (-1, 1, 0) if (dr, db) != (0, 0)]
 FAR = [(dr, db) for dr in (-3, 3) for db in (-1, 0, 1)]
 CORNERS = [(dr, db) for dr in (-1, 1) for db in (-1, 1)]
 
@@ -89,7 +89,7 @@
         return (lax.rem(r + (dr + NREG), NREG), lax.rem(b + (db + NBLK), NBLK))
 
     bar = pltpu.get_barrier_semaphore()
-    for off in NEAR + FAR:
+    for off in FAR + NEAR:
         pl.semaphore_signal(bar, inc=1, device_id=dev(*off), device_id_type=MESH)
 
     loads = []
@@ -160,7 +160,7 @@
                         ysend[side, n, CROWS + (i * 2 + h) * 2 + j] = rn[x + 2, h, 8 + y : 9 + y, :]
             return 0
 
-        lax.fori_loop(0, CH, root, 0, unroll=2)
+        lax.fori_loop(0, CH, root, 0, unroll=3)
         if n == 0:
             pl.semaphore_wait(bar, len(NEAR) + len(FAR))
         ymsg.append([
@@ -306,8 +306,8 @@
             cp.wait()
         unpack(n)
         run(own_setup, max(CH * n - 1, 1), CH * n + CH - 1, CH)
-    run(first, 2, 22, 7)
-    run(second, 3, 21, 6)
+    run(first, 2, 22, 10)
+    run(second, 3, 21, 9)
     run(resid, 4, 20, 8)
 
     for cp in xmsg + cmsg:
@@ -378,12 +378,12 @@
             )
 
     residual_sums()
-    rmsg = [
-        remote(RM.at[7:10, 1], RM.at[7 - 3 * dr : 10 - 3 * dr, 1 - db], (dr, db)) for dr, db in NEAR
-    ]
+    rmsg = []
     for dr, db in FAR:
         s, t = (9, 0) if dr > 0 else (7, 16)
         rmsg.append(remote(RM.at[s, 1], RM.at[t, 1 - db], (dr, db)))
+    for dr, db in NEAR:
+        rmsg.append(remote(RM.at[7:10, 1], RM.at[7 - 3 * dr : 10 - 3 * dr, 1 - db], (dr, db)))
 
     def upack(x, _):
         for h in range(2):
@@ -392,7 +392,7 @@
                 usend[1, (x * 2 + h) * 3 + j] = UB[x + XO, h, 2 + j, 7:8, :]
         return 0
 
-    lax.fori_loop(0, XL, upack, 0)
+    lax.fori_loop(0, XL, upack, 0, unroll=4)
     for n, (dr, db) in enumerate(CORNERS):
         for p in range(2):
             X = XO + (p if dr < 0 else XL - 2 + p)
@@ -451,7 +451,7 @@
                 UB[x + XO, h, 5 + j, 7:8, :] = urecv[1, (x * 2 + h) * 3 + j] * above
         return 0
 
-    lax.fori_loop(0, XL, uunpack, 0)
+    lax.fori_loop(0, XL, uunpack, 0, unroll=4)
     def u_halo():
         for X, n, i, side in (
             (0, 0, 0, left), (1, 0, 1, left), (2, 0, 2, left),
@@ -549,9 +549,9 @@
 
     add(0)
     add(1)
-    run(third, -2, 26, 7)
-    run(fourth, -1, 25, 13)
-    run(fifth, 0, XL, 8)
+    run(third, -2, 26, 14)
+    run(fourth, -1, 25, 26)
+    run(fifth, 0, XL, 24)
 
 
 def vmem(*shape):

time: 35.4 us -> 34.5 us (0.975)
  Pallas kernels: 34.2 us -> 33.3 us
    pallas_call x1, Pallas kernels: 34.2 us -> 33.3 us  [shards(): pl.pallas_call(kernel, name='vcycle', out_shape=pltpu.VMEM(right_side.sha...]
where the time goes in v6:
time: 34.5 us
  Pallas kernels  33.3 us (97%)
  local copies, waits for them, and re-layouts  1.15 us (3%)
    pallas_call x1, Pallas kernels, shards(): pl.pallas_call(kernel, name='vcycle', out_shape=pltpu.VMEM(right_side.sha...  33.3 us
    unnamed x1, local copies, waits for them, and re-layouts  1.15 us

profile of v6, /device:TPU:1, one launch (start us, length us, event | category | flops | bytes accessed | tf_op | source)
XLA Modules:
  0.0 34.5 jit_solution(13816460018843901582)
XLA Ops:
  0.0 33.3 %vcycle.1 = f32[24,64,256]{2,1,0:T(8,128)S(1)} custom-call(f32[24,64,256]{2,1,0:T(8,128)} %k_ref.1, s32[24,64,256]{2,1,0:T(8,128)} %solid_ref.1, f32[24,64,256]{2,1,0:T(8,128)} %rs_ref.1), custom_call_target="tpu_custom_call" | custom-call | tf_op jit(solution)/shard_map/vcycle/pallas_call | solution.py:581
  33.3 1.1 %copy.5 = f32[24,64,256]{2,1,0:T(8,128)} copy(f32[24,64,256]{2,1,0:T(8,128)S(1)} %vcycle.1) | data formatting | bytes 3145728
